TPU v7x, 32 devices: a whole 2x2x4 slice. The times are simulated.
32 devices in a mesh: samples: 8 (over z, y), params: 4 (over x, core).
Axes of the slice: x: 2, y: 2, z: 4, core: 2. Of those that a mesh axis runs over, the one named last changes fastest.
Arguments:
- occupations: int32 [512, 152], P('samples'), may hold values from 0 to 1, as said below
- connection_counts: int32 [512], P('samples'), may hold values from 0 to 3072, as said below
- connection_orbitals: int32 [4, 24576], P(None, ('samples', 'params')), may hold values from 0 to 151, as said below
- connection_elements: float32 [2, 24576], P(None, ('samples', 'params')), may hold values from -2 to 2
- laser_step: int32 [], replicated, may hold values from 0 to 3999
- first_weight: bfloat16 [152, 1024], replicated, may hold values from -4 to 4
- first_bias: float32 [1024], replicated, may hold values from -3 to 3
- second_weight: bfloat16 [1024, 256], P('params'), may hold values from -1.25 to 1.25
- readout: float32 [2, 256], replicated, may hold values from -0.375 to 0.375
Outputs:
- local_energy: float32 [2, 512], P(None, 'samples')
- change: float32 [2, 512], P(None, 'samples')
Inputs may be any that keep to these rules, and one draw needn't show every extreme that they name: `occupations`: each row has exactly 76 ones. `connection_counts`: the connections of block b of 64 consecutive samples fill the first slots q of that block in order of sample; the counts of a block sum to at most 3072, and to exactly 3072 in some block. `connection_orbitals`: the 4 orbitals of a slot are distinct; unused slots hold arbitrary orbitals in the range.
All inputs are finite; a program needn't handle non-finite values.
Results may differ from a plain program's by a relative error of at most 0.0099.
Values may be sent and summed in bfloat16 or wider, within the bound.
No kernel may reach another device: no remote copies, remote signals or barrier semaphores. Data moves between devices by JAX's collectives and lax.ppermute only.
A program may use at most 64 MiB of HBM per device.

v0:
```python
import functools
import math

import jax
import jax.numpy as jnp
from jax import lax
from jax.experimental import pallas as pl
from jax.experimental.pallas import tpu as pltpu
from jax.sharding import Mesh, PartitionSpec as P

ITERS = 2


FIELD_SCALE = 0.8
FIELD_RATE = 0.0123
DIAG_SHIFT = 0.01
F32 = jnp.float32
BF16 = jnp.bfloat16
ROWS = 256
COLLECT_WEIGHT = 1e10
NEAR_WEIGHT = 1e10
VMEM_LIMIT = 48 * 1024 * 1024


def dot(a, b, dims):
    return lax.dot_general(a, b, (dims, ((), ())), preferred_element_type=F32)


def split(x):
    high = lax.reduce_precision(x, 8, 7)
    return high.astype(BF16), (x - high).astype(BF16)


def parts(x):
    high = x.astype(BF16)
    rest = x - high.astype(F32)
    middle = rest.astype(BF16)
    return high, middle, (rest - middle.astype(F32)).astype(BF16)


def iota(shape, dim):
    return lax.broadcasted_iota(jnp.int32, shape, dim)


def call(kernel, count, out_shape, scratch=(), name=None, copies=False, flops=0, transcendentals=0):
    vmem = pl.BlockSpec(memory_space=pltpu.VMEM)
    far = pl.BlockSpec(memory_space=pltpu.HBM)
    return pl.pallas_call(
        kernel,
        out_shape=out_shape,
        in_specs=[far if copies else vmem] * count,
        out_specs=jax.tree.map(lambda _: vmem, out_shape),
        scratch_shapes=scratch,
        compiler_params=pltpu.CompilerParams(vmem_limit_bytes=VMEM_LIMIT),
        cost_estimate=pl.CostEstimate(
            flops=int(flops),
            transcendentals=int(transcendentals),
            bytes_accessed=sum(x.size * x.dtype.itemsize for x in jax.tree.leaves(out_shape)),
        ),
        name=name,
    )


def slot_hidden_kernel(
    spread,
    counts_hbm,
    orbitals_hbm,
    occ_hbm,
    w1_hbm,
    bias_hbm,
    elements_hbm,
    readout_hbm,
    own_hbm,
    hidden_ref,
    owner_ref,
    elements_ref,
    w1_ref,
    bias_ref,
    readout_ref,
    own_ref,
    occupied_ref,
    counts_ref,
    orbitals_ref,
    occ_ref,
    sems,
):
    here, orbitals = occ_ref.shape
    updates, slots = orbitals_ref.shape
    pairs = (
        (counts_hbm, counts_ref),
        (occ_hbm, occ_ref),
        (w1_hbm, w1_ref),
        (bias_hbm, bias_ref),
        (orbitals_hbm, orbitals_ref),
        (elements_hbm, elements_ref),
        (readout_hbm, readout_ref),
        (own_hbm, own_ref),
    )
    copies = [pltpu.make_async_copy(a, b, sems.at[i]) for i, (a, b) in enumerate(pairs)]
    for copy in copies:
        copy.start()
    chip, core = lax.axis_index("chip"), lax.axis_index("core")
    place = chip * 2 + core
    copies[0].wait()
    counts = counts_ref[...].astype(F32)
    row, col = iota((here, here), 0), iota((here, here), 1)
    ends = jnp.sum(jnp.where(col <= row, counts, 0.0), axis=1, keepdims=True)
    starts = jnp.sum(jnp.where(col < row, counts, 0.0), axis=1, keepdims=True)
    positions = (place + spread * iota((1, slots), 1)).astype(F32)
    owner = jnp.where((starts <= positions) & (positions < ends), 1.0, 0.0).astype(BF16)
    owner_ref[...] = owner
    copies[1].wait()
    occupied = occ_ref[...].astype(F32).astype(BF16)
    occupied_ref[...] = occupied
    copies[2].wait()
    copies[3].wait()
    w1 = w1_ref[...]
    bias = bias_ref[...]
    hidden_ref[slots:, :] = jnp.tanh(dot(occupied, w1, ((1,), (0,))) + bias).astype(BF16)
    copies[4].wait()
    for start in range(0, slots, ROWS):
        stop = min(start + ROWS, slots)
        parent_occ = dot(occupied, owner[:, start:stop], ((0,), (0,)))
        columns = iota((orbitals, stop - start), 0)
        flipped = columns == orbitals_ref[0:1, start:stop]
        for u in range(1, updates):
            flipped = flipped | (columns == orbitals_ref[u : u + 1, start:stop])
        slot_occ = jnp.where(flipped, 1.0 - parent_occ, parent_occ).astype(BF16)
        pre = dot(slot_occ, w1, ((0,), (0,))) + bias
        hidden_ref[start:stop, :] = jnp.tanh(pre).astype(BF16)
    copies[5].wait()
    copies[6].wait()
    copies[7].wait()


def sine_cosine(x):
    turns = jnp.floor(x * (2.0 / math.pi) + 0.5)
    rest = ((x - turns * 1.5703125) - turns * 4.837512969970703125e-4) - turns * 7.549789948768648e-8
    square = rest * rest
    sine = (-1.9515295891e-4 * square + 8.3321608736e-3) * square - 1.6666654611e-1
    sine = rest + rest * square * sine
    cosine = (2.443315711809948e-5 * square - 1.388731625493765e-3) * square + 4.166664568298827e-2
    cosine = 1.0 - 0.5 * square + square * square * cosine
    quarter = turns.astype(jnp.int32) & 3
    odd = (quarter & 1) == 1
    high_sine = jnp.where(odd, cosine, sine)
    high_cosine = jnp.where(odd, sine, cosine)
    sine = jnp.where(quarter >= 2, -high_sine, high_sine)
    cosine = jnp.where((quarter == 1) | (quarter == 2), -high_cosine, high_cosine)
    return sine, cosine


def slot_energy_kernel(
    shifts, field_ref, hidden_ref, owner_ref, elements_ref, readout_ref, *refs
):
    shard_refs, (send_ref, second_ref) = refs[: len(shifts)], refs[len(shifts) :]
    here, slots = owner_ref.shape
    chips = lax.axis_size("chip")
    chip, core = lax.axis_index("chip"), lax.axis_index("core")
    for (step, other), shard in zip(shifts, shard_refs):
        rows = shard.shape[0]
        source = lax.rem(chip + chips - step, chips) * 2 + (core ^ other)
        second_ref[pl.ds(pl.multiple_of(source * rows, rows), rows), :] = shard[...]
    mid = jnp.tanh(dot(second_ref[...], hidden_ref[...], ((0,), (1,))))
    readout = readout_ref[...].T
    logs_re = jnp.sum(mid * readout[:, 0:1], axis=0, keepdims=True)
    logs_im = jnp.sum(mid * readout[:, 1:2], axis=0, keepdims=True)
    owner = owner_ref[...]
    own = jnp.concatenate(parts(logs_re[:, slots:]) + parts(logs_im[:, slots:]), axis=0)
    parent = dot(own, owner, ((1,), (0,)))
    diff_re = logs_re[:, :slots] - (parent[0:1] + parent[1:2] + parent[2:3])
    diff_im = logs_im[:, :slots] - (parent[3:4] + parent[4:5] + parent[5:6])
    used = jnp.sum(owner.astype(F32), axis=0, keepdims=True) > 0.0
    weight = elements_ref[0:1, :] + field_ref[...] * elements_ref[1:2, :]
    scale = weight * jnp.exp(diff_re)
    sine, cosine = sine_cosine(diff_im)
    contrib_re = jnp.where(used, scale * cosine, 0.0)
    contrib_im = jnp.where(used, scale * sine, 0.0)
    contrib = jnp.concatenate(parts(contrib_re) + parts(contrib_im), axis=0)
    sums = dot(contrib, owner, ((1,), (1,)))
    partial_re = sums[0:1] + sums[1:2] + sums[2:3]
    partial_im = sums[3:4] + sums[4:5] + sums[5:6]
    row = jnp.concatenate([partial_re, partial_im], axis=1)
    send_ref[...] = jnp.broadcast_to(row[None], send_ref.shape)


def collect(entries, spread, received_ref):
    peers, here = received_ref.shape[0], received_ref.shape[2] // 2
    block = lax.axis_index("samples")
    out_re, out_im = [], []
    for entry in entries:
        first = lax.rem((block ^ entry) * spread + peers // 2, peers)
        row = received_ref[first]
        for k in range(1, spread):
            row = row + received_ref[first + k]
        out_re.append(row[:, :here])
        out_im.append(row[:, here:])
    return jnp.concatenate([jnp.concatenate(out_re, axis=1), jnp.concatenate(out_im, axis=1)], axis=0)


def collect_kernel(entries, spread, received_ref, after_ref, energy_ref):
    del after_ref
    energy_ref[...] = collect(entries, spread, received_ref)


def sample_values(packed_ref, w1_ref, bias_ref, second_ref, readout_ref, size):
    hidden = jnp.tanh(sample_pre(packed_ref, w1_ref, bias_ref, size)).astype(BF16)
    mid = jnp.tanh(dot(second_ref[...], hidden, ((0,), (1,))))
    slope = 1.0 - mid * mid
    readout = readout_ref[...].T
    return hidden, slope * readout[:, 0:1], slope * readout[:, 1:2]


def pack_kernel(mine_ref, moved_ref, after_ref, packed_ref):
    del after_ref
    blocks, here, orbitals = mine_ref.shape
    full = packed_ref.shape[1]
    pieces = [mine_ref[k] for k in range(blocks)] + [moved_ref[k] for k in range(blocks)]
    rest = orbitals - full
    for k, piece in enumerate(pieces):
        packed_ref[k * here : (k + 1) * here, :] = piece[:, :full]
    rests = [piece[:, full:].astype(F32) for piece in pieces]
    rests.append(jnp.zeros((here, full - rest * len(pieces)), F32))
    packed_ref[len(pieces) * here :, :] = jnp.concatenate(rests, axis=1).astype(BF16)


def sample_pre(packed_ref, w1_ref, bias_ref, size):
    full = packed_ref.shape[1]
    here = packed_ref.shape[0] - size
    rest = w1_ref.shape[0] - full
    tail = packed_ref[size:, :].astype(F32)
    rests = [tail[:, k * rest : (k + 1) * rest] for k in range(size // here)]
    tail = jnp.concatenate(rests, axis=0).astype(BF16)
    pre = dot(packed_ref[:size, :], w1_ref[:full, :], ((1,), (0,)))
    return pre + dot(tail, w1_ref[full:, :], ((1,), (0,))) + bias_ref[...]


def put(overlap_ref, overlap):
    size = overlap.shape[0]
    high = overlap.astype(BF16)
    overlap_ref[:size, :] = high
    overlap_ref[size : 2 * size, :] = (overlap - high.astype(F32)).astype(BF16)
    overlap_ref[2 * size :, :] = high


def near_half_kernel(
    packed_ref, w1_ref, bias_ref, second_ref, readout_ref, w1_again, hidden_ref, near_ref, re_ref, im_ref
):
    w1_again[...] = w1_ref[...]
    size = hidden_ref.shape[0]
    hidden, re_ref[...], im_ref[...] = sample_values(packed_ref, w1_ref, bias_ref, second_ref, readout_ref, size)
    hidden_ref[...] = hidden
    put(near_ref, dot(hidden, hidden, ((1,), (1,))))


def far_half_kernel(
    packed_ref,
    w1_ref,
    bias_ref,
    second_ref,
    readout_ref,
    hidden_ref,
    near_far_ref,
    far_near_ref,
    far_ref,
    re_ref,
    im_ref,
):
    size = hidden_ref.shape[0]
    hidden, re_ref[...], im_ref[...] = sample_values(packed_ref, w1_ref, bias_ref, second_ref, readout_ref, size)
    near = hidden_ref[...]
    put(near_far_ref, dot(near, hidden, ((1,), (1,))))
    put(far_near_ref, dot(hidden, near, ((1,), (1,))))
    put(far_ref, dot(hidden, hidden, ((1,), (1,))))


def solve(energy, gram):
    total = energy.shape[1]
    centered = energy - jnp.mean(energy, axis=1, keepdims=True)
    res_c = jnp.concatenate([centered[1:2], -centered[0:1]], axis=0) / total
    res_y = gram(res_c)
    dir_c, dir_y = res_c, res_y
    norm_now = full_sum(res_c * res_y)
    cross, square = norm_now, full_sum(res_y * res_y)
    change = jnp.zeros_like(res_y)
    for turn in range(ITERS):
        alpha = norm_now / (square / total + DIAG_SHIFT * cross)
        change = change + alpha * dir_y
        if turn + 1 < ITERS:
            img_c = dir_y / total + DIAG_SHIFT * dir_c
            img_y = gram(dir_y) / total + DIAG_SHIFT * dir_y
            res_c = res_c - alpha * img_c
            res_y = res_y - alpha * img_y
            norm_next = full_sum(res_c * res_y)
            mixed = full_sum(res_c * dir_y) + full_sum(dir_c * res_y)
            squares = full_sum(res_y * res_y), full_sum(res_y * dir_y)
            beta = norm_next / norm_now
            cross = norm_next + beta * mixed + beta * beta * cross
            square = squares[0] + 2.0 * beta * squares[1] + beta * beta * square
            dir_c = res_c + beta * dir_c
            dir_y = res_y + beta * dir_y
            norm_now = norm_next
    return change


def full_sum(x):
    return jnp.sum(jnp.sum(x, axis=1, keepdims=True), axis=0, keepdims=True)


def project(lifted, slope_re, slope_im):
    raw = jnp.concatenate(
        [jnp.sum(lifted * slope_re, axis=0, keepdims=True), jnp.sum(lifted * slope_im, axis=0, keepdims=True)],
        axis=0,
    )
    return raw - jnp.mean(raw, axis=1, keepdims=True)


def solve_kernel(
    energy_ref,
    near_ref,
    near_re_ref,
    near_im_ref,
    near_far_ref,
    far_near_ref,
    far_ref,
    far_re_ref,
    far_im_ref,
    local_ref,
    change_ref,
):
    width = local_ref.shape[1]
    half = near_ref.shape[1]
    energy = energy_ref[...]
    local_ref[...] = energy[:, :width]

    def scaled(c, re_ref, im_ref):
        back = re_ref[...] * c[0:1] + im_ref[...] * c[1:2]
        high = back.astype(BF16)
        low = (back - high.astype(F32)).astype(BF16)
        return jnp.concatenate([high, high, low], axis=1)

    def raw(lifted, re_ref, im_ref):
        re = jnp.sum(lifted * re_ref[...], axis=0, keepdims=True)
        return jnp.concatenate([re, jnp.sum(lifted * im_ref[...], axis=0, keepdims=True)], axis=0)

    def gram(c):
        near = scaled(c[:, :half], near_re_ref, near_im_ref)
        far = scaled(c[:, half:], far_re_ref, far_im_ref)
        to_near = dot(near, near_ref[...], ((1,), (0,))) + dot(far, far_near_ref[...], ((1,), (0,)))
        to_far = dot(near, near_far_ref[...], ((1,), (0,))) + dot(far, far_ref[...], ((1,), (0,)))
        both = jnp.concatenate(
            [raw(to_near, near_re_ref, near_im_ref), raw(to_far, far_re_ref, far_im_ref)], axis=1
        )
        return both - jnp.mean(both, axis=1, keepdims=True)

    change_ref[...] = solve(energy, gram)[:, :width]


def wide_solve(energy, occ_stack, first_weight, bias_row, second, readout):
    here = occ_stack.shape[1]
    occupied = occ_stack.reshape(-1, occ_stack.shape[2])
    pre = dot(occupied, first_weight, ((1,), (0,))) + bias_row
    hidden = jnp.tanh(pre).astype(BF16)
    mid = jnp.tanh(dot(second, hidden, ((0,), (1,))))
    slope = 1.0 - mid * mid
    slope_re = slope * readout[0][:, None]
    slope_im = slope * readout[1][:, None]

    def gram(c):
        high, low = split(slope_re * c[0:1] + slope_im * c[1:2])
        high, low = split(dot(high, hidden, ((1,), (0,))) + dot(low, hidden, ((1,), (0,))))
        lifted = dot(high, hidden, ((1,), (1,))) + dot(low, hidden, ((1,), (1,)))
        return project(lifted, slope_re, slope_im)

    return energy[:, :here], solve(energy, gram)[:, :here]


def swap(x, axis, bit):
    return lax.ppermute(x, axis, [(i, i ^ bit) for i in range(lax.axis_size(axis))])


def shift(x, axis, step):
    size = lax.axis_size(axis)
    return lax.ppermute(x, axis, [(i, (i + step) % size) for i in range(size)])


def exchange_all(send):
    peers = send.shape[0]
    return lax.all_to_all(
        send,
        ("samples", "chip", "core"),
        0,
        0,
        axis_index_groups=[[(k + peers // 2) % peers for k in range(peers)]],
        tiled=True,
    )


def powers(size):
    return [1 << k for k in reversed(range((size - 1).bit_length()))]


def body(
    occupations,
    connection_counts,
    connection_orbitals,
    connection_elements,
    laser_step,
    first_weight,
    first_bias,
    second_weight,
    readout,
):
    here, orbitals = occupations.shape
    slots = connection_orbitals.shape[1]
    wide, narrow = first_weight.shape[1], second_weight.shape[1]
    chips = lax.axis_size("chip")
    spread = chips * lax.axis_size("core")
    blocks = lax.axis_size("samples")
    total = here * blocks
    bias_row = first_bias[None, :]
    field = FIELD_SCALE * jnp.sin(FIELD_RATE * laser_step.astype(F32)[None, None])

    bits = powers(blocks)
    bits = bits[-1:] + bits[:-1]
    entries = [0]
    for bit in bits:
        entries = entries + [e ^ bit for e in entries]
    moved = swap(occupations.astype(BF16)[None], "samples", bits[0])

    shifts, shards = [], []
    for step in range(1, chips):
        shifts.append((step, 0))
        shards.append(shift(second_weight, "chip", step))
    shifts.append((0, 1))
    shards.append(shift(second_weight, "core", 1))

    hidden, owner, elements, w1, bias, readout_near, own_shard, occupied = call(
        functools.partial(slot_hidden_kernel, spread),
        8,
        (
            jax.ShapeDtypeStruct((slots + here, wide), BF16),
            jax.ShapeDtypeStruct((here, slots), BF16),
            jax.ShapeDtypeStruct(connection_elements.shape, F32),
            jax.ShapeDtypeStruct(first_weight.shape, BF16),
            jax.ShapeDtypeStruct(bias_row.shape, F32),
            jax.ShapeDtypeStruct(readout.shape, F32),
            jax.ShapeDtypeStruct(second_weight.shape, BF16),
            jax.ShapeDtypeStruct(occupations.shape, BF16),
        ),
        [
            pltpu.VMEM((1, here), jnp.int32),
            pltpu.VMEM(connection_orbitals.shape, jnp.int32),
            pltpu.VMEM(occupations.shape, jnp.int32),
            pltpu.SemaphoreType.DMA((8,)),
        ],
        name="slot_hidden",
        copies=True,
        flops=2 * (slots + here) * orbitals * wide,
        transcendentals=(slots + here) * wide,
    )(
        *(
            pltpu.with_memory_space_constraint(x, pltpu.HBM)
            for x in (
                connection_counts[None, :],
                connection_orbitals,
                occupations,
                first_weight,
                bias_row,
                connection_elements,
                readout,
                second_weight,
            )
        ),
    )
    relayed, occupied, field = lax.optimization_barrier((shards[: chips - 1], occupied, field))
    for step in range(1, chips):
        shifts.append((step, 1))
        shards.append(shift(relayed[step - 1], "core", 1))
    shifts.append((0, 0))
    stack = jnp.concatenate([occupied[None], moved], axis=0)
    moved = swap(stack, "samples", bits[1])

    send, second = call(
        functools.partial(slot_energy_kernel, tuple(shifts)),
        5 + len(shifts),
        (
            jax.ShapeDtypeStruct((blocks * spread, 1, 2 * here), F32),
            jax.ShapeDtypeStruct((wide, narrow), BF16),
        ),
        name="slot_energy",
        flops=2 * (slots + here) * wide * narrow,
        transcendentals=(slots + here) * narrow,
    )(field, hidden, owner, elements, readout_near, *shards, own_shard)
    received = exchange_all(send)

    def collected(after):
        return call(
            functools.partial(collect_kernel, entries, spread),
            2,
            jax.ShapeDtypeStruct((2, total), F32),
            name="collect",
            flops=COLLECT_WEIGHT,
        )(received, after)

    for bit in bits[2:-1]:
        stack = jnp.concatenate([stack, moved], axis=0)
        moved = swap(stack, "samples", bit)
    if total > wide:
        stack = jnp.concatenate([stack, moved], axis=0)
        stack = jnp.concatenate([stack, swap(stack, "samples", bits[-1])], axis=0)
        return wide_solve(collected(stack), stack, first_weight, bias_row, second, readout)

    half = total // 2
    weights = (w1, bias, second, readout_near)
    full = orbitals // 128 * 128
    packed = call(
        pack_kernel,
        3,
        jax.ShapeDtypeStruct((half + here, full), BF16),
        name="pack",
    )(stack, moved, second)
    far_packed = swap(packed, "samples", bits[-1])
    block = jax.ShapeDtypeStruct((3 * half, half), BF16)
    slopes = (jax.ShapeDtypeStruct((narrow, half), F32),) * 2
    w1, near_hidden, *near = call(
        near_half_kernel,
        5,
        (jax.ShapeDtypeStruct(w1.shape, BF16), jax.ShapeDtypeStruct((half, wide), BF16), block) + slopes,
        name="near_half",
        flops=NEAR_WEIGHT,
        transcendentals=half * (wide + narrow),
    )(packed, *weights)
    far = call(
        far_half_kernel,
        6,
        (block,) * 3 + slopes,
        name="far_half",
        flops=2 * half * wide * (orbitals + narrow + 3 * half),
        transcendentals=half * (wide + narrow),
    )(far_packed, w1, *weights[1:], near_hidden)
    return call(
        solve_kernel,
        9,
        (jax.ShapeDtypeStruct((2, here), F32),) * 2,
        name="solve",
        flops=ITERS * 6 * total * total * narrow,
    )(collected(far[0]), *near, *far)


def solution(mesh):
    blocks, spread = mesh.shape["samples"], mesh.shape["params"]
    fine = Mesh(mesh.devices.reshape(blocks, spread // 2, 2), ("samples", "chip", "core"))
    return jax.shard_map(
        body,
        mesh=fine,
        in_specs=(
            P("samples", None),
            P("samples"),
            P(None, ("samples", "chip", "core")),
            P(None, ("samples", "chip", "core")),
            P(),
            P(),
            P(),
            P(("chip", "core"), None),
            P(),
        ),
        out_specs=(P(None, "samples"), P(None, "samples")),
        check_vma=False,
    )
```

profile of v0, /device:TPU:0, one launch (start us, length us, event | category | flops | bytes accessed | tf_op | source)
XLA Modules:
  0.0 26.2 jit_solution(4422569466776097816)
XLA Ops:
  0.6 3.0 %collective-permute-start = (bf16[256,256]{1,0:T(8,128)(2,1)}, bf16[256,256]{1,0:T(8,128)(2,1)S(1)}, u32[]{:S(2)}, u32[]{:S(2)}) collective-permute-start(bf16[256,256]{1,0:T(8,128)(2,1)} %own_hbm.1), channel_id=1, source_target_pairs={{0,2},{2,0},{1,3},{3,1},{4,6},{6,4},{5,7},{7,5},{8,10},{10,8},{9,1... | collective-permute-start | bytes 393224 | tf_op jit(solution)/shard_map/ppermute | solution.py:384
  3.6 0.0 collective-permute-start.1
  3.6 0.8 %convert_bitcast_fusion = bf16[1,64,152]{2,1,0:T(8,128)(2,1)S(1)} fusion(s32[64,152]{1,0:T(8,128)} %occ_hbm.1), kind=kLoop, calls=%fused_computation.1 | loop fusion | flops 9728 | bytes 58368 | tf_op jit(solution)/shard_map/broadcast_in_dim | solution.py:429
  4.5 1.5 %collective-permute-start.3 = (bf16[1,64,152]{2,1,0:T(8,128)(2,1)S(1)}, bf16[1,64,152]{2,1,0:T(8,128)(2,1)S(1)}, u32[]{:S(2)}, u32[]{:S(2)}) collective-permute-start(bf16[1,64,152]{2,1,0:T(8,128)(2,1)S(1)} %convert_bitcast_fusion), channel_id=1, source_target_pairs={{0,4},{4,0},{8,12},{12,8},{16,20},{20,16},{24,28},{28,24},{1,5},{5... | collective-permute-start | bytes 58376 | tf_op jit(solution)/shard_map/ppermute | solution.py:379
  6.0 2.6 %slot_hidden.1 = (bf16[832,1024]{1,0:T(8,128)(2,1)S(1)}, bf16[64,768]{1,0:T(8,128)(2,1)S(1)}, f32[2,768]{1,0:T(2,128)S(1)}, bf16[152,1024]{1,0:T(8,128)(2,1)S(1)...) custom-call(s32[1,64]{1,0:T(1,128)} %bitcast.8, ...), custom_call_target="tpu_custom_call" | custom-call | flops 258998272 | bytes 2276352 | tf_op jit(solution)/shard_map/slot_hidden/pallas_call | solution.py:438
  9.4 0.0 collective-permute-done.refs_0_
  9.4 0.3 %collective-permute-start.2 = (bf16[256,256]{1,0:T(8,128)(2,1)S(1)}, bf16[256,256]{1,0:T(8,128)(2,1)S(1)}, u32[]{:S(2)}, u32[]{:S(2)}) collective-permute-start(bf16[256,256]{1,0:T(8,128)(2,1)S(1)} %collective-permute-done.refs_0_), channel_id=1, source_target_pairs={{0,1},{1,0},{2,3},{3,2},{4,5},{5,4},{6,7},{7,6},{8,9},{9,8},{10,11... | collective-permute-start | bytes 393224 | tf_op jit(solution)/shard_map/ppermute | solution.py:384
  9.7 0.0 collective-permute-done.3
  9.7 2.6 %collective-permute-start.4 = (bf16[2,64,152]{2,1,0:T(8,128)(2,1)S(1)}, bf16[2,64,152]{2,1,0:T(8,128)(2,1)S(1)}, u32[]{:S(2)}, u32[]{:S(2)}) collective-permute-start(bf16[2,64,152]{2,1,0:T(8,128)(2,1)S(1)} %pad_maximum_fusion.mine_ref), channel_id=1, source_target_pairs={{0,16},{4,20},{8,24},{12,28},{16,0},{20,4},{24,8},{28,12},{1,17},{... | collective-permute-start | bytes 116744 | tf_op jit(solution)/shard_map/ppermute | solution.py:379
  12.4 0.0 collective-permute-done.1.refs_1_
  12.4 0.0 collective-permute-done.2.refs_2_
  12.4 1.9 %slot_energy.1 = (f32[32,1,128]{2,1,0:T(1,128)}, bf16[1024,256]{1,0:T(8,128)(2,1)S(1)}) custom-call(f32[1,1]{1,0:T(1,128)} %bitcast.2.field_ref, bf16[832,1024]{1,0:T(8,128)(2,1)S(1)} %get-tuple-element.27.hidden_ref, bf16[64,768]{1,0:T(8,128)(2,1)S(1)} %get-tuple-element.28.owner_ref, f32[2,768]{1,0:T(2,128)S(1)} %get-tuple-element.29.elements_ref, ...), custom_call_target="tpu_custom_call" | custom-call | flops 436207616 | bytes 540672 | tf_op jit(solution)/shard_map/slot_energy/pallas_call | solution.py:484
  14.3 2.5 %all-to-all-start = ((f32[32,1,128]{2,1,0:T(1,128)}), f32[32,1,128]{2,1,0:T(1,128)S(1)}, u32[]{:S(2)}, u32[]{:S(2)}) async-start(f32[32,1,128]{2,1,0:T(1,128)} %get-tuple-element.33), calls=%async_computation | async-start | bytes 32768 | tf_op jit(solution)/shard_map/all_to_all | solution.py:389
  16.8 0.0 collective-permute-done.4.moved_ref
  16.8 0.1 pack.1.packed_ref
  16.9 1.8 %collective-permute-start.5 = (bf16[320,128]{1,0:T(8,128)(2,1)S(1)}, bf16[320,128]{1,0:T(8,128)(2,1)S(1)}, u32[]{:S(2)}, u32[]{:S(2)}) collective-permute-start(bf16[320,128]{1,0:T(8,128)(2,1)S(1)} %pack.1.packed_ref), channel_id=1, source_target_pairs={{0,8},{4,12},{8,0},{12,4},{16,24},{20,28},{24,16},{28,20},{1,9},{5... | collective-permute-start | bytes 245768 | tf_op jit(solution)/shard_map/ppermute | solution.py:379
  18.7 0.9 %near_half.1 = (bf16[152,1024]{1,0:T(8,128)(2,1)S(1)}, bf16[256,1024]{1,0:T(8,128)(2,1)S(1)}, bf16[768,256]{1,0:T(8,128)(2,1)S(1)}, f32[256,256]{1,0:T(8,128)S(1)}, f32[256,256]{1,0:T(8,128)S(1)}) custom-call(bf16[320,128]{1,0:T(8,128)(2,1)S(1)} %pack.1.packed_ref, bf16[152,1024]{1,0:T(8,128)(2,1)S(1)} %get-tuple-element.36.w1_ref, ...), custom_call_target="tpu_custom_call" | custom-call | flops 10000000000 | bytes 1753088 | tf_op jit(solution)/shard_map/near_half/pallas_call | solution.py:526
  19.6 2.1 %collective-permute-done.5.packed_ref = bf16[320,128]{1,0:T(8,128)(2,1)S(1)} collective-permute-done((bf16[320,128]{1,0:T(8,128)(2,1)S(1)}, bf16[320,128]{1,0:T(8,128)(2,1)S(1)}, u32[]{:S(2)}, u32[]{:S(2)}) %collective-permute-start.5) | collective-permute-done | bytes 81952 | tf_op jit(solution)/shard_map/ppermute | solution.py:379
  21.7 1.2 %far_half.1 = (bf16[768,256]{1,0:T(8,128)(2,1)S(1)}, bf16[768,256]{1,0:T(8,128)(2,1)S(1)}, bf16[768,256]{1,0:T(8,128)(2,1)S(1)}, f32[256,256]{1,0:T(8,128)S(1)}, f32[256,256]{1,0:T(8,128)S(1)}) custom-call(bf16[320,128]{1,0:T(8,128)(2,1)S(1)} %collective-permute-done.5.packed_ref, bf16[152,1024]{1,0:T(8,128)(2,1)S(1)} %get-tuple-element.38.w1_ref, ...), custom_call_target="tpu_custom_call" | custom-call | flops 616562688 | bytes 1703936 | tf_op jit(solution)/shard_map/far_half/pallas_call | solution.py:534
  22.8 1.2 %all-to-all-done.received_ref = f32[32,1,128]{2,1,0:T(1,128)S(1)} async-done(((f32[32,1,128]{2,1,0:T(1,128)}), f32[32,1,128]{2,1,0:T(1,128)S(1)}, u32[]{:S(2)}, u32[]{:S(2)}) %all-to-all-start) | async-done | bytes 16416 | tf_op jit(solution)/shard_map/all_to_all | solution.py:389
  24.0 0.1 collect.1.energy_ref
  24.1 2.1 %solve.1 = (f32[2,64]{1,0:T(2,128)}, f32[2,64]{1,0:T(2,128)}) custom-call(f32[2,512]{1,0:T(2,128)S(1)} %collect.1.energy_ref, bf16[768,256]{1,0:T(8,128)(2,1)S(1)} %get-tuple-element.41.near_ref, f32[256,256]{1,0:T(8,128)S(1)} %get-tuple-element.42.near_re_ref, f32[256,256]{1,0:T(8,128)S(1)} %get-tuple-element.43.near_im_ref, ...), custom_call_target="tpu_custom_call" | custom-call | flops 805306368 | bytes 1024 | tf_op jit(solution)/shard_map/solve/pallas_call | solution.py:542
  (1 shorter events, 0.0 us)
Async XLA Ops:
  0.6 8.8 %collective-permute-start = (bf16[256,256]{1,0:T(8,128)(2,1)}, bf16[256,256]{1,0:T(8,128)(2,1)S(1)}, u32[]{:S(2)}, u32[]{:S(2)}) collective-permute-start(bf16[256,256]{1,0:T(8,128)(2,1)} %own_hbm.1), channel_id=1, source_target_pairs={{0,2},{2,0},{1,3},{3,1},{4,6},{6,4},{5,7},{7,5},{8,10},{10,8},{9,1... | collective-permute-start | bytes 393224 | tf_op jit(solution)/shard_map/ppermute | solution.py:384
  3.6 8.7 %collective-permute-start.1 = (bf16[256,256]{1,0:T(8,128)(2,1)}, bf16[256,256]{1,0:T(8,128)(2,1)S(1)}, u32[]{:S(2)}, u32[]{:S(2)}) collective-permute-start(bf16[256,256]{1,0:T(8,128)(2,1)} %own_hbm.1), channel_id=1, source_target_pairs={{0,1},{1,0},{2,3},{3,2},{4,5},{5,4},{6,7},{7,6},{8,9},{9,8},{10,11... | collective-permute-start | bytes 393224 | tf_op jit(solution)/shard_map/ppermute | solution.py:384
  4.5 5.2 %collective-permute-start.3 = (bf16[1,64,152]{2,1,0:T(8,128)(2,1)S(1)}, bf16[1,64,152]{2,1,0:T(8,128)(2,1)S(1)}, u32[]{:S(2)}, u32[]{:S(2)}) collective-permute-start(bf16[1,64,152]{2,1,0:T(8,128)(2,1)S(1)} %convert_bitcast_fusion), channel_id=1, source_target_pairs={{0,4},{4,0},{8,12},{12,8},{16,20},{20,16},{24,28},{28,24},{1,5},{5... | collective-permute-start | bytes 58376 | tf_op jit(solution)/shard_map/ppermute | solution.py:379
  9.4 3.0 %collective-permute-start.2 = (bf16[256,256]{1,0:T(8,128)(2,1)S(1)}, bf16[256,256]{1,0:T(8,128)(2,1)S(1)}, u32[]{:S(2)}, u32[]{:S(2)}) collective-permute-start(bf16[256,256]{1,0:T(8,128)(2,1)S(1)} %collective-permute-done.refs_0_), channel_id=1, source_target_pairs={{0,1},{1,0},{2,3},{3,2},{4,5},{5,4},{6,7},{7,6},{8,9},{9,8},{10,11... | collective-permute-start | bytes 393224 | tf_op jit(solution)/shard_map/ppermute | solution.py:384
  9.7 7.1 %collective-permute-start.4 = (bf16[2,64,152]{2,1,0:T(8,128)(2,1)S(1)}, bf16[2,64,152]{2,1,0:T(8,128)(2,1)S(1)}, u32[]{:S(2)}, u32[]{:S(2)}) collective-permute-start(bf16[2,64,152]{2,1,0:T(8,128)(2,1)S(1)} %pad_maximum_fusion.mine_ref), channel_id=1, source_target_pairs={{0,16},{4,20},{8,24},{12,28},{16,0},{20,4},{24,8},{28,12},{1,17},{... | collective-permute-start | bytes 116744 | tf_op jit(solution)/shard_map/ppermute | solution.py:379
  14.3 9.7 %all-to-all-start = ((f32[32,1,128]{2,1,0:T(1,128)}), f32[32,1,128]{2,1,0:T(1,128)S(1)}, u32[]{:S(2)}, u32[]{:S(2)}) async-start(f32[32,1,128]{2,1,0:T(1,128)} %get-tuple-element.33), calls=%async_computation | async-start | bytes 32768 | tf_op jit(solution)/shard_map/all_to_all | solution.py:389
  16.9 4.8 %collective-permute-start.5 = (bf16[320,128]{1,0:T(8,128)(2,1)S(1)}, bf16[320,128]{1,0:T(8,128)(2,1)S(1)}, u32[]{:S(2)}, u32[]{:S(2)}) collective-permute-start(bf16[320,128]{1,0:T(8,128)(2,1)S(1)} %pack.1.packed_ref), channel_id=1, source_target_pairs={{0,8},{4,12},{8,0},{12,4},{16,24},{20,28},{24,16},{28,20},{1,9},{5... | collective-permute-start | bytes 245768 | tf_op jit(solution)/shard_map/ppermute | solution.py:379
where the time goes:
time: 26.4 us; the launch traced here: 26.2 us
  starting transfers between devices  11.7 us (44%)
  Pallas kernels  8.94 us (34%)
  waiting for transfers between devices  3.28 us (12%)
  between operations  1.42 us (5%)
  other arithmetic  0.86 us (3%)
    ppermute x3, starting transfers between devices, swap(): lax.ppermute(x, axis, [(i, i ^ bit) for i in range(lax.axis_size(axis))])  5.96 us
    ppermute x3, starting transfers between devices, shift(): return lax.ppermute(x, axis, [(i, (i + step) % size) for i in range(size)])  3.3 us
    pallas_call x1, Pallas kernels, body(): call(functools.partial(slot_hidden_kernel, spread), 8, (jax.ShapeDtypeStr...  2.64 us
    all_to_all x1, starting transfers between devices, exchange_all(): lax.all_to_all(send, ('samples', 'chip', 'core'), 0, 0, axis_index_groups...  2.46 us
    pallas_call x1, Pallas kernels, body(): call(solve_kernel, 9, (jax.ShapeDtypeStruct((2, here), F32),) * 2, name='...  2.15 us
    ppermute x3, waiting for transfers between devices, swap(): lax.ppermute(x, axis, [(i, i ^ bit) for i in range(lax.axis_size(axis))])  2.12 us
    pallas_call x1, Pallas kernels, body(): call(functools.partial(slot_energy_kernel, tuple(shifts)), 5 + len(shifts...  1.93 us
    all_to_all x1, waiting for transfers between devices, exchange_all(): lax.all_to_all(send, ('samples', 'chip', 'core'), 0, 0, axis_index_groups...  1.16 us
  transfers between devices with their start and end apart: 7, of which 2 were waited for; matrix products, arithmetic and copies ran while one was open for 3% of the time, Pallas kernels for 26%

commit v1 on v0

--- a/solution.py
+++ b/solution.py
@@ -426,7 +426,7 @@
     entries = [0]
     for bit in bits:
         entries = entries + [e ^ bit for e in entries]
-    moved = swap(occupations.astype(BF16)[None], "samples", bits[0])
+    moved = swap(occupations[None], "samples", bits[0])
 
     shifts, shards = [], []
     for step in range(1, chips):
@@ -478,7 +478,7 @@
         shifts.append((step, 1))
         shards.append(shift(relayed[step - 1], "core", 1))
     shifts.append((0, 0))
-    stack = jnp.concatenate([occupied[None], moved], axis=0)
+    stack = jnp.concatenate([occupied[None], moved.astype(BF16)], axis=0)
     moved = swap(stack, "samples", bits[1])
 
     send, second = call(

time: 26.4 us -> 26.4 us (level)
  other arithmetic: 0.86 us -> 0.02 us
  starting transfers between devices: 11.7 us -> 12.5 us
    broadcast_in_dim x1 -> x0, other arithmetic: 0.85 us -> none  [body(): moved = swap(occupations.astype(BF16)[None], 'samples', bits[0])]
    all_to_all x1, starting transfers between devices: 2.46 us -> 3.23 us  [exchange_all(): lax.all_to_all(send, ('samples', 'chip', 'core'), 0, 0, axis_index_groups...]
  transfers between devices with their start and end apart: 7 -> 7, of which waited for: 2 -> 2; matrix products, arithmetic and copies ran while one was open for 3% -> 0% of each run, Pallas kernels for 26% -> 26%
where the time goes in v1:
time: 26.4 us; the launch traced here: 26.2 us
  starting transfers between devices  12.5 us (47%)
  Pallas kernels  8.96 us (34%)
  waiting for transfers between devices  3.25 us (12%)
  between operations  1.43 us (5%)
    ppermute x3, starting transfers between devices, swap(): lax.ppermute(x, axis, [(i, i ^ bit) for i in range(lax.axis_size(axis))])  6.01 us
    ppermute x3, starting transfers between devices, shift(): return lax.ppermute(x, axis, [(i, (i + step) % size) for i in range(size)])  3.31 us
    all_to_all x1, starting transfers between devices, exchange_all(): lax.all_to_all(send, ('samples', 'chip', 'core'), 0, 0, axis_index_groups...  3.23 us
    pallas_call x1, Pallas kernels, body(): call(functools.partial(slot_hidden_kernel, spread), 8, (jax.ShapeDtypeStr...  2.65 us
    pallas_call x1, Pallas kernels, body(): call(solve_kernel, 9, (jax.ShapeDtypeStruct((2, here), F32),) * 2, name='...  2.16 us
    ppermute x3, waiting for transfers between devices, swap(): lax.ppermute(x, axis, [(i, i ^ bit) for i in range(lax.axis_size(axis))])  2.12 us
    pallas_call x1, Pallas kernels, body(): call(functools.partial(slot_energy_kernel, tuple(shifts)), 5 + len(shifts...  1.93 us
    pallas_call x1, Pallas kernels, body(): call(far_half_kernel, 6, (block,) * 3 + slopes, name='far_half', flops=2...  1.15 us
  transfers between devices with their start and end apart: 7, of which 2 were waited for; matrix products, arithmetic and copies ran while one was open for 0% of the time, Pallas kernels for 26%

profile of v1, /device:TPU:0, one launch (start us, length us, event | category | flops | bytes accessed | tf_op | source)
XLA Modules:
  0.0 26.2 jit_solution(2347789524033417349)
XLA Ops:
  0.6 3.0 %collective-permute-start = (bf16[256,256]{1,0:T(8,128)(2,1)}, bf16[256,256]{1,0:T(8,128)(2,1)S(1)}, u32[]{:S(2)}, u32[]{:S(2)}) collective-permute-start(bf16[256,256]{1,0:T(8,128)(2,1)} %own_hbm.1), channel_id=1, source_target_pairs={{0,2},{2,0},{1,3},{3,1},{4,6},{6,4},{5,7},{7,5},{8,10},{10,8},{9,1... | collective-permute-start | bytes 393224 | tf_op jit(solution)/shard_map/ppermute | solution.py:384
  3.6 0.0 collective-permute-start.1
  3.6 1.5 %collective-permute-start.3 = (s32[1,64,152]{2,1,0:T(8,128)}, s32[1,64,152]{2,1,0:T(8,128)S(1)}, u32[]{:S(2)}, u32[]{:S(2)}) collective-permute-start(s32[1,64,152]{2,1,0:T(8,128)} %bitcast.6), channel_id=1, source_target_pairs={{0,4},{4,0},{8,12},{12,8},{16,20},{20,16},{24,28},{28,24},{1,5},{5... | collective-permute-start | bytes 116744 | tf_op jit(solution)/shard_map/ppermute | solution.py:379
  5.9 2.6 %slot_hidden.1 = (bf16[832,1024]{1,0:T(8,128)(2,1)S(1)}, bf16[64,768]{1,0:T(8,128)(2,1)S(1)}, f32[2,768]{1,0:T(2,128)S(1)}, bf16[152,1024]{1,0:T(8,128)(2,1)S(1)...) custom-call(s32[1,64]{1,0:T(1,128)} %bitcast.8, ...), custom_call_target="tpu_custom_call" | custom-call | flops 258998272 | bytes 2276352 | tf_op jit(solution)/shard_map/slot_hidden/pallas_call | solution.py:438
  8.5 0.0 collective-permute-done.refs_0_
  8.6 0.3 %collective-permute-start.2 = (bf16[256,256]{1,0:T(8,128)(2,1)S(1)}, bf16[256,256]{1,0:T(8,128)(2,1)S(1)}, u32[]{:S(2)}, u32[]{:S(2)}) collective-permute-start(bf16[256,256]{1,0:T(8,128)(2,1)S(1)} %collective-permute-done.refs_0_), channel_id=1, source_target_pairs={{0,1},{1,0},{2,3},{3,2},{4,5},{5,4},{6,7},{7,6},{8,9},{9,8},{10,11... | collective-permute-start | bytes 393224 | tf_op jit(solution)/shard_map/ppermute | solution.py:384
  8.9 0.0 collective-permute-done.3
  8.9 2.7 %collective-permute-start.4 = (bf16[2,64,152]{2,1,0:T(8,128)(2,1)S(1)}, bf16[2,64,152]{2,1,0:T(8,128)(2,1)S(1)}, u32[]{:S(2)}, u32[]{:S(2)}) collective-permute-start(bf16[2,64,152]{2,1,0:T(8,128)(2,1)S(1)} %pad_maximum_fusion.mine_ref), channel_id=1, source_target_pairs={{0,16},{4,20},{8,24},{12,28},{16,0},{20,4},{24,8},{28,12},{1,17},{... | collective-permute-start | bytes 116744 | tf_op jit(solution)/shard_map/ppermute | solution.py:379
  11.5 0.0 collective-permute-done.1.refs_1_
  11.5 0.0 collective-permute-done.2.refs_2_
  11.6 1.9 %slot_energy.1 = (f32[32,1,128]{2,1,0:T(1,128)}, bf16[1024,256]{1,0:T(8,128)(2,1)S(1)}) custom-call(f32[1,1]{1,0:T(1,128)} %bitcast.2.field_ref, bf16[832,1024]{1,0:T(8,128)(2,1)S(1)} %get-tuple-element.27.hidden_ref, bf16[64,768]{1,0:T(8,128)(2,1)S(1)} %get-tuple-element.28.owner_ref, f32[2,768]{1,0:T(2,128)S(1)} %get-tuple-element.29.elements_ref, ...), custom_call_target="tpu_custom_call" | custom-call | flops 436207616 | bytes 540672 | tf_op jit(solution)/shard_map/slot_energy/pallas_call | solution.py:484
  13.5 3.2 %all-to-all-start = ((f32[32,1,128]{2,1,0:T(1,128)}), f32[32,1,128]{2,1,0:T(1,128)S(1)}, u32[]{:S(2)}, u32[]{:S(2)}) async-start(f32[32,1,128]{2,1,0:T(1,128)} %get-tuple-element.33), calls=%async_computation | async-start | bytes 32768 | tf_op jit(solution)/shard_map/all_to_all | solution.py:389
  16.7 0.0 collective-permute-done.4.moved_ref
  16.7 0.1 pack.1.packed_ref
  16.8 1.8 %collective-permute-start.5 = (bf16[320,128]{1,0:T(8,128)(2,1)S(1)}, bf16[320,128]{1,0:T(8,128)(2,1)S(1)}, u32[]{:S(2)}, u32[]{:S(2)}) collective-permute-start(bf16[320,128]{1,0:T(8,128)(2,1)S(1)} %pack.1.packed_ref), channel_id=1, source_target_pairs={{0,8},{4,12},{8,0},{12,4},{16,24},{20,28},{24,16},{28,20},{1,9},{5... | collective-permute-start | bytes 245768 | tf_op jit(solution)/shard_map/ppermute | solution.py:379
  18.7 0.9 %near_half.1 = (bf16[152,1024]{1,0:T(8,128)(2,1)S(1)}, bf16[256,1024]{1,0:T(8,128)(2,1)S(1)}, bf16[768,256]{1,0:T(8,128)(2,1)S(1)}, f32[256,256]{1,0:T(8,128)S(1)}, f32[256,256]{1,0:T(8,128)S(1)}) custom-call(bf16[320,128]{1,0:T(8,128)(2,1)S(1)} %pack.1.packed_ref, bf16[152,1024]{1,0:T(8,128)(2,1)S(1)} %get-tuple-element.36.w1_ref, ...), custom_call_target="tpu_custom_call" | custom-call | flops 10000000000 | bytes 1753088 | tf_op jit(solution)/shard_map/near_half/pallas_call | solution.py:526
  19.6 2.1 %collective-permute-done.5.packed_ref = bf16[320,128]{1,0:T(8,128)(2,1)S(1)} collective-permute-done((bf16[320,128]{1,0:T(8,128)(2,1)S(1)}, bf16[320,128]{1,0:T(8,128)(2,1)S(1)}, u32[]{:S(2)}, u32[]{:S(2)}) %collective-permute-start.5) | collective-permute-done | bytes 81952 | tf_op jit(solution)/shard_map/ppermute | solution.py:379
  21.7 1.2 %far_half.1 = (bf16[768,256]{1,0:T(8,128)(2,1)S(1)}, bf16[768,256]{1,0:T(8,128)(2,1)S(1)}, bf16[768,256]{1,0:T(8,128)(2,1)S(1)}, f32[256,256]{1,0:T(8,128)S(1)}, f32[256,256]{1,0:T(8,128)S(1)}) custom-call(bf16[320,128]{1,0:T(8,128)(2,1)S(1)} %collective-permute-done.5.packed_ref, bf16[152,1024]{1,0:T(8,128)(2,1)S(1)} %get-tuple-element.38.w1_ref, ...), custom_call_target="tpu_custom_call" | custom-call | flops 616562688 | bytes 1703936 | tf_op jit(solution)/shard_map/far_half/pallas_call | solution.py:534
  22.8 1.1 %all-to-all-done.received_ref = f32[32,1,128]{2,1,0:T(1,128)S(1)} async-done(((f32[32,1,128]{2,1,0:T(1,128)}), f32[32,1,128]{2,1,0:T(1,128)S(1)}, u32[]{:S(2)}, u32[]{:S(2)}) %all-to-all-start) | async-done | bytes 16416 | tf_op jit(solution)/shard_map/all_to_all | solution.py:389
  23.9 0.1 collect.1.energy_ref
  24.0 2.2 %solve.1 = (f32[2,64]{1,0:T(2,128)}, f32[2,64]{1,0:T(2,128)}) custom-call(f32[2,512]{1,0:T(2,128)S(1)} %collect.1.energy_ref, bf16[768,256]{1,0:T(8,128)(2,1)S(1)} %get-tuple-element.41.near_ref, f32[256,256]{1,0:T(8,128)S(1)} %get-tuple-element.42.near_re_ref, f32[256,256]{1,0:T(8,128)S(1)} %get-tuple-element.43.near_im_ref, ...), custom_call_target="tpu_custom_call" | custom-call | flops 805306368 | bytes 1024 | tf_op jit(solution)/shard_map/solve/pallas_call | solution.py:542
  (2 shorter events, 0.0 us)
Async XLA Ops:
  0.6 7.9 %collective-permute-start = (bf16[256,256]{1,0:T(8,128)(2,1)}, bf16[256,256]{1,0:T(8,128)(2,1)S(1)}, u32[]{:S(2)}, u32[]{:S(2)}) collective-permute-start(bf16[256,256]{1,0:T(8,128)(2,1)} %own_hbm.1), channel_id=1, source_target_pairs={{0,2},{2,0},{1,3},{3,1},{4,6},{6,4},{5,7},{7,5},{8,10},{10,8},{9,1... | collective-permute-start | bytes 393224 | tf_op jit(solution)/shard_map/ppermute | solution.py:384
  3.6 7.9 %collective-permute-start.1 = (bf16[256,256]{1,0:T(8,128)(2,1)}, bf16[256,256]{1,0:T(8,128)(2,1)S(1)}, u32[]{:S(2)}, u32[]{:S(2)}) collective-permute-start(bf16[256,256]{1,0:T(8,128)(2,1)} %own_hbm.1), channel_id=1, source_target_pairs={{0,1},{1,0},{2,3},{3,2},{4,5},{5,4},{6,7},{7,6},{8,9},{9,8},{10,11... | collective-permute-start | bytes 393224 | tf_op jit(solution)/shard_map/ppermute | solution.py:384
  3.6 5.2 %collective-permute-start.3 = (s32[1,64,152]{2,1,0:T(8,128)}, s32[1,64,152]{2,1,0:T(8,128)S(1)}, u32[]{:S(2)}, u32[]{:S(2)}) collective-permute-start(s32[1,64,152]{2,1,0:T(8,128)} %bitcast.6), channel_id=1, source_target_pairs={{0,4},{4,0},{8,12},{12,8},{16,20},{20,16},{24,28},{28,24},{1,5},{5... | collective-permute-start | bytes 116744 | tf_op jit(solution)/shard_map/ppermute | solution.py:379
  8.6 3.0 %collective-permute-start.2 = (bf16[256,256]{1,0:T(8,128)(2,1)S(1)}, bf16[256,256]{1,0:T(8,128)(2,1)S(1)}, u32[]{:S(2)}, u32[]{:S(2)}) collective-permute-start(bf16[256,256]{1,0:T(8,128)(2,1)S(1)} %collective-permute-done.refs_0_), channel_id=1, source_target_pairs={{0,1},{1,0},{2,3},{3,2},{4,5},{5,4},{6,7},{7,6},{8,9},{9,8},{10,11... | collective-permute-start | bytes 393224 | tf_op jit(solution)/shard_map/ppermute | solution.py:384
  8.9 7.8 %collective-permute-start.4 = (bf16[2,64,152]{2,1,0:T(8,128)(2,1)S(1)}, bf16[2,64,152]{2,1,0:T(8,128)(2,1)S(1)}, u32[]{:S(2)}, u32[]{:S(2)}) collective-permute-start(bf16[2,64,152]{2,1,0:T(8,128)(2,1)S(1)} %pad_maximum_fusion.mine_ref), channel_id=1, source_target_pairs={{0,16},{4,20},{8,24},{12,28},{16,0},{20,4},{24,8},{28,12},{1,17},{... | collective-permute-start | bytes 116744 | tf_op jit(solution)/shard_map/ppermute | solution.py:379
  13.5 10.5 %all-to-all-start = ((f32[32,1,128]{2,1,0:T(1,128)}), f32[32,1,128]{2,1,0:T(1,128)S(1)}, u32[]{:S(2)}, u32[]{:S(2)}) async-start(f32[32,1,128]{2,1,0:T(1,128)} %get-tuple-element.33), calls=%async_computation | async-start | bytes 32768 | tf_op jit(solution)/shard_map/all_to_all | solution.py:389
  16.8 4.8 %collective-permute-start.5 = (bf16[320,128]{1,0:T(8,128)(2,1)S(1)}, bf16[320,128]{1,0:T(8,128)(2,1)S(1)}, u32[]{:S(2)}, u32[]{:S(2)}) collective-permute-start(bf16[320,128]{1,0:T(8,128)(2,1)S(1)} %pack.1.packed_ref), channel_id=1, source_target_pairs={{0,8},{4,12},{8,0},{12,4},{16,24},{20,28},{24,16},{28,20},{1,9},{5... | collective-permute-start | bytes 245768 | tf_op jit(solution)/shard_map/ppermute | solution.py:379

commit v2 on v1

--- a/solution.py
+++ b/solution.py
@@ -316,7 +316,9 @@
 
 
 def solve_kernel(
-    energy_ref,
+    entries,
+    spread,
+    received_ref,
     near_ref,
     near_re_ref,
     near_im_ref,
@@ -330,7 +332,7 @@
 ):
     width = local_ref.shape[1]
     half = near_ref.shape[1]
-    energy = energy_ref[...]
+    energy = collect(entries, spread, received_ref)
     local_ref[...] = energy[:, :width]
 
     def scaled(c, re_ref, im_ref):
@@ -540,12 +542,12 @@
         transcendentals=half * (wide + narrow),
     )(far_packed, w1, *weights[1:], near_hidden)
     return call(
-        solve_kernel,
+        functools.partial(solve_kernel, entries, spread),
         9,
         (jax.ShapeDtypeStruct((2, here), F32),) * 2,
         name="solve",
-        flops=ITERS * 6 * total * total * narrow,
-    )(collected(far[0]), *near, *far)
+        flops=COLLECT_WEIGHT,
+    )(received, *near, *far)
 
 
 def solution(mesh):

time: 26.4 us -> 26.4 us (level)
    pallas_call x2 -> x1, Pallas kernels: 2.26 us -> 2.21 us  [body(): call(functools.partial(solve_kernel, entries, spread), 9, (jax.ShapeDtype...]
where the time goes in v2:
time: 26.4 us; the launch traced here: 26.2 us
  starting transfers between devices  12.5 us (47%)
  Pallas kernels  8.91 us (34%)
  waiting for transfers between devices  3.25 us (12%)
  between operations  1.43 us (5%)
    ppermute x3, starting transfers between devices, swap(): lax.ppermute(x, axis, [(i, i ^ bit) for i in range(lax.axis_size(axis))])  6.01 us
    ppermute x3, starting transfers between devices, shift(): return lax.ppermute(x, axis, [(i, (i + step) % size) for i in range(size)])  3.31 us
    all_to_all x1, starting transfers between devices, exchange_all(): lax.all_to_all(send, ('samples', 'chip', 'core'), 0, 0, axis_index_groups...  3.23 us
    pallas_call x1, Pallas kernels, body(): call(functools.partial(slot_hidden_kernel, spread), 8, (jax.ShapeDtypeStr...  2.65 us
    pallas_call x1, Pallas kernels, body(): call(functools.partial(solve_kernel, entries, spread), 9, (jax.ShapeDtype...  2.21 us
    ppermute x3, waiting for transfers between devices, swap(): lax.ppermute(x, axis, [(i, i ^ bit) for i in range(lax.axis_size(axis))])  2.12 us
    pallas_call x1, Pallas kernels, body(): call(functools.partial(slot_energy_kernel, tuple(shifts)), 5 + len(shifts...  1.93 us
    pallas_call x1, Pallas kernels, body(): call(far_half_kernel, 6, (block,) * 3 + slopes, name='far_half', flops=2...  1.15 us
  transfers between devices with their start and end apart: 7, of which 2 were waited for; matrix products, arithmetic and copies ran while one was open for 0% of the time, Pallas kernels for 26%

profile of v2, /device:TPU:0, one launch (start us, length us, event | category | flops | bytes accessed | tf_op | source)
XLA Modules:
  0.0 26.2 jit_solution(8603445300566029210)
XLA Ops:
  0.6 3.0 %collective-permute-start = (bf16[256,256]{1,0:T(8,128)(2,1)}, bf16[256,256]{1,0:T(8,128)(2,1)S(1)}, u32[]{:S(2)}, u32[]{:S(2)}) collective-permute-start(bf16[256,256]{1,0:T(8,128)(2,1)} %own_hbm.1), channel_id=1, source_target_pairs={{0,2},{2,0},{1,3},{3,1},{4,6},{6,4},{5,7},{7,5},{8,10},{10,8},{9,1... | collective-permute-start | bytes 393224 | tf_op jit(solution)/shard_map/ppermute | solution.py:386
  3.6 0.0 collective-permute-start.1
  3.6 1.5 %collective-permute-start.3 = (s32[1,64,152]{2,1,0:T(8,128)}, s32[1,64,152]{2,1,0:T(8,128)S(1)}, u32[]{:S(2)}, u32[]{:S(2)}) collective-permute-start(s32[1,64,152]{2,1,0:T(8,128)} %bitcast.6), channel_id=1, source_target_pairs={{0,4},{4,0},{8,12},{12,8},{16,20},{20,16},{24,28},{28,24},{1,5},{5... | collective-permute-start | bytes 116744 | tf_op jit(solution)/shard_map/ppermute | solution.py:381
  5.9 2.6 %slot_hidden.1 = (bf16[832,1024]{1,0:T(8,128)(2,1)S(1)}, bf16[64,768]{1,0:T(8,128)(2,1)S(1)}, f32[2,768]{1,0:T(2,128)S(1)}, bf16[152,1024]{1,0:T(8,128)(2,1)S(1)...) custom-call(s32[1,64]{1,0:T(1,128)} %bitcast.8, ...), custom_call_target="tpu_custom_call" | custom-call | flops 258998272 | bytes 2276352 | tf_op jit(solution)/shard_map/slot_hidden/pallas_call | solution.py:440
  8.5 0.0 collective-permute-done.refs_0_
  8.6 0.3 %collective-permute-start.2 = (bf16[256,256]{1,0:T(8,128)(2,1)S(1)}, bf16[256,256]{1,0:T(8,128)(2,1)S(1)}, u32[]{:S(2)}, u32[]{:S(2)}) collective-permute-start(bf16[256,256]{1,0:T(8,128)(2,1)S(1)} %collective-permute-done.refs_0_), channel_id=1, source_target_pairs={{0,1},{1,0},{2,3},{3,2},{4,5},{5,4},{6,7},{7,6},{8,9},{9,8},{10,11... | collective-permute-start | bytes 393224 | tf_op jit(solution)/shard_map/ppermute | solution.py:386
  8.9 0.0 collective-permute-done.3
  8.9 2.7 %collective-permute-start.4 = (bf16[2,64,152]{2,1,0:T(8,128)(2,1)S(1)}, bf16[2,64,152]{2,1,0:T(8,128)(2,1)S(1)}, u32[]{:S(2)}, u32[]{:S(2)}) collective-permute-start(bf16[2,64,152]{2,1,0:T(8,128)(2,1)S(1)} %pad_maximum_fusion.mine_ref), channel_id=1, source_target_pairs={{0,16},{4,20},{8,24},{12,28},{16,0},{20,4},{24,8},{28,12},{1,17},{... | collective-permute-start | bytes 116744 | tf_op jit(solution)/shard_map/ppermute | solution.py:381
  11.5 0.0 collective-permute-done.1.refs_1_
  11.5 0.0 collective-permute-done.2.refs_2_
  11.6 1.9 %slot_energy.1 = (f32[32,1,128]{2,1,0:T(1,128)}, bf16[1024,256]{1,0:T(8,128)(2,1)S(1)}) custom-call(f32[1,1]{1,0:T(1,128)} %bitcast.2.field_ref, bf16[832,1024]{1,0:T(8,128)(2,1)S(1)} %get-tuple-element.27.hidden_ref, bf16[64,768]{1,0:T(8,128)(2,1)S(1)} %get-tuple-element.28.owner_ref, f32[2,768]{1,0:T(2,128)S(1)} %get-tuple-element.29.elements_ref, ...), custom_call_target="tpu_custom_call" | custom-call | flops 436207616 | bytes 540672 | tf_op jit(solution)/shard_map/slot_energy/pallas_call | solution.py:486
  13.5 3.2 %all-to-all-start = ((f32[32,1,128]{2,1,0:T(1,128)}), f32[32,1,128]{2,1,0:T(1,128)S(1)}, u32[]{:S(2)}, u32[]{:S(2)}) async-start(f32[32,1,128]{2,1,0:T(1,128)} %get-tuple-element.33), calls=%async_computation | async-start | bytes 32768 | tf_op jit(solution)/shard_map/all_to_all | solution.py:391
  16.7 0.0 collective-permute-done.4.moved_ref
  16.7 0.1 pack.1.packed_ref
  16.8 1.8 %collective-permute-start.5 = (bf16[320,128]{1,0:T(8,128)(2,1)S(1)}, bf16[320,128]{1,0:T(8,128)(2,1)S(1)}, u32[]{:S(2)}, u32[]{:S(2)}) collective-permute-start(bf16[320,128]{1,0:T(8,128)(2,1)S(1)} %pack.1.packed_ref), channel_id=1, source_target_pairs={{0,8},{4,12},{8,0},{12,4},{16,24},{20,28},{24,16},{28,20},{1,9},{5... | collective-permute-start | bytes 245768 | tf_op jit(solution)/shard_map/ppermute | solution.py:381
  18.7 0.9 %near_half.1 = (bf16[152,1024]{1,0:T(8,128)(2,1)S(1)}, bf16[256,1024]{1,0:T(8,128)(2,1)S(1)}, bf16[768,256]{1,0:T(8,128)(2,1)S(1)}, f32[256,256]{1,0:T(8,128)S(1)}, f32[256,256]{1,0:T(8,128)S(1)}) custom-call(bf16[320,128]{1,0:T(8,128)(2,1)S(1)} %pack.1.packed_ref, bf16[152,1024]{1,0:T(8,128)(2,1)S(1)} %get-tuple-element.36.w1_ref, ...), custom_call_target="tpu_custom_call" | custom-call | flops 10000000000 | bytes 1753088 | tf_op jit(solution)/shard_map/near_half/pallas_call | solution.py:528
  19.6 2.1 %collective-permute-done.5.packed_ref = bf16[320,128]{1,0:T(8,128)(2,1)S(1)} collective-permute-done((bf16[320,128]{1,0:T(8,128)(2,1)S(1)}, bf16[320,128]{1,0:T(8,128)(2,1)S(1)}, u32[]{:S(2)}, u32[]{:S(2)}) %collective-permute-start.5) | collective-permute-done | bytes 81952 | tf_op jit(solution)/shard_map/ppermute | solution.py:381
  21.7 1.2 %far_half.1 = (bf16[768,256]{1,0:T(8,128)(2,1)S(1)}, bf16[768,256]{1,0:T(8,128)(2,1)S(1)}, bf16[768,256]{1,0:T(8,128)(2,1)S(1)}, f32[256,256]{1,0:T(8,128)S(1)}, f32[256,256]{1,0:T(8,128)S(1)}) custom-call(bf16[320,128]{1,0:T(8,128)(2,1)S(1)} %collective-permute-done.5.packed_ref, bf16[152,1024]{1,0:T(8,128)(2,1)S(1)} %get-tuple-element.41.w1_ref, ...), custom_call_target="tpu_custom_call" | custom-call | flops 616562688 | bytes 1703936 | tf_op jit(solution)/shard_map/far_half/pallas_call | solution.py:536
  22.8 1.1 %all-to-all-done.received_ref = f32[32,1,128]{2,1,0:T(1,128)S(1)} async-done(((f32[32,1,128]{2,1,0:T(1,128)}), f32[32,1,128]{2,1,0:T(1,128)S(1)}, u32[]{:S(2)}, u32[]{:S(2)}) %all-to-all-start) | async-done | bytes 16416 | tf_op jit(solution)/shard_map/all_to_all | solution.py:391
  23.9 2.2 %solve.1 = (f32[2,64]{1,0:T(2,128)}, f32[2,64]{1,0:T(2,128)}) custom-call(f32[32,1,128]{2,1,0:T(1,128)S(1)} %all-to-all-done.received_ref, bf16[768,256]{1,0:T(8,128)(2,1)S(1)} %get-tuple-element.38.near_ref, f32[256,256]{1,0:T(8,128)S(1)} %get-tuple-element.39.near_re_ref, f32[256,256]{1,0:T(8,128)S(1)} %get-tuple-element.40.near_im_ref, ...), custom_call_target="tpu_custom_call" | custom-call | flops 10000000000 | bytes 1024 | tf_op jit(solution)/shard_map/solve/pallas_call | solution.py:544
  (2 shorter events, 0.0 us)
Async XLA Ops:
  0.6 7.9 %collective-permute-start = (bf16[256,256]{1,0:T(8,128)(2,1)}, bf16[256,256]{1,0:T(8,128)(2,1)S(1)}, u32[]{:S(2)}, u32[]{:S(2)}) collective-permute-start(bf16[256,256]{1,0:T(8,128)(2,1)} %own_hbm.1), channel_id=1, source_target_pairs={{0,2},{2,0},{1,3},{3,1},{4,6},{6,4},{5,7},{7,5},{8,10},{10,8},{9,1... | collective-permute-start | bytes 393224 | tf_op jit(solution)/shard_map/ppermute | solution.py:386
  3.6 7.9 %collective-permute-start.1 = (bf16[256,256]{1,0:T(8,128)(2,1)}, bf16[256,256]{1,0:T(8,128)(2,1)S(1)}, u32[]{:S(2)}, u32[]{:S(2)}) collective-permute-start(bf16[256,256]{1,0:T(8,128)(2,1)} %own_hbm.1), channel_id=1, source_target_pairs={{0,1},{1,0},{2,3},{3,2},{4,5},{5,4},{6,7},{7,6},{8,9},{9,8},{10,11... | collective-permute-start | bytes 393224 | tf_op jit(solution)/shard_map/ppermute | solution.py:386
  3.6 5.2 %collective-permute-start.3 = (s32[1,64,152]{2,1,0:T(8,128)}, s32[1,64,152]{2,1,0:T(8,128)S(1)}, u32[]{:S(2)}, u32[]{:S(2)}) collective-permute-start(s32[1,64,152]{2,1,0:T(8,128)} %bitcast.6), channel_id=1, source_target_pairs={{0,4},{4,0},{8,12},{12,8},{16,20},{20,16},{24,28},{28,24},{1,5},{5... | collective-permute-start | bytes 116744 | tf_op jit(solution)/shard_map/ppermute | solution.py:381
  8.6 3.0 %collective-permute-start.2 = (bf16[256,256]{1,0:T(8,128)(2,1)S(1)}, bf16[256,256]{1,0:T(8,128)(2,1)S(1)}, u32[]{:S(2)}, u32[]{:S(2)}) collective-permute-start(bf16[256,256]{1,0:T(8,128)(2,1)S(1)} %collective-permute-done.refs_0_), channel_id=1, source_target_pairs={{0,1},{1,0},{2,3},{3,2},{4,5},{5,4},{6,7},{7,6},{8,9},{9,8},{10,11... | collective-permute-start | bytes 393224 | tf_op jit(solution)/shard_map/ppermute | solution.py:386
  8.9 7.8 %collective-permute-start.4 = (bf16[2,64,152]{2,1,0:T(8,128)(2,1)S(1)}, bf16[2,64,152]{2,1,0:T(8,128)(2,1)S(1)}, u32[]{:S(2)}, u32[]{:S(2)}) collective-permute-start(bf16[2,64,152]{2,1,0:T(8,128)(2,1)S(1)} %pad_maximum_fusion.mine_ref), channel_id=1, source_target_pairs={{0,16},{4,20},{8,24},{12,28},{16,0},{20,4},{24,8},{28,12},{1,17},{... | collective-permute-start | bytes 116744 | tf_op jit(solution)/shard_map/ppermute | solution.py:381
  13.5 10.5 %all-to-all-start = ((f32[32,1,128]{2,1,0:T(1,128)}), f32[32,1,128]{2,1,0:T(1,128)S(1)}, u32[]{:S(2)}, u32[]{:S(2)}) async-start(f32[32,1,128]{2,1,0:T(1,128)} %get-tuple-element.33), calls=%async_computation | async-start | bytes 32768 | tf_op jit(solution)/shard_map/all_to_all | solution.py:391
  16.8 4.8 %collective-permute-start.5 = (bf16[320,128]{1,0:T(8,128)(2,1)S(1)}, bf16[320,128]{1,0:T(8,128)(2,1)S(1)}, u32[]{:S(2)}, u32[]{:S(2)}) collective-permute-start(bf16[320,128]{1,0:T(8,128)(2,1)S(1)} %pack.1.packed_ref), channel_id=1, source_target_pairs={{0,8},{4,12},{8,0},{12,4},{16,24},{20,28},{24,16},{28,20},{1,9},{5... | collective-permute-start | bytes 245768 | tf_op jit(solution)/shard_map/ppermute | solution.py:381

commit v3 on v1

--- a/solution.py
+++ b/solution.py
@@ -16,7 +16,7 @@
 DIAG_SHIFT = 0.01
 F32 = jnp.float32
 BF16 = jnp.bfloat16
-ROWS = 256
+ROWS = 768
 COLLECT_WEIGHT = 1e10
 NEAR_WEIGHT = 1e10
 VMEM_LIMIT = 48 * 1024 * 1024

time: 26.4 us -> 26.4 us (level)
  starting transfers between devices: 12.5 us -> 12.9 us
  Pallas kernels: 8.96 us -> 8.58 us
    all_to_all x1, starting transfers between devices: 3.23 us -> 3.62 us  [exchange_all(): lax.all_to_all(send, ('samples', 'chip', 'core'), 0, 0, axis_index_groups...]
    pallas_call x1, Pallas kernels: 2.65 us -> 2.27 us  [body(): call(functools.partial(slot_hidden_kernel, spread), 8, (jax.ShapeDtypeStr...]
  transfers between devices with their start and end apart: 7 -> 7, of which waited for: 2 -> 2; matrix products, arithmetic and copies ran while one was open for 0% -> 0% of each run, Pallas kernels for 26% -> 24%
where the time goes in v3:
time: 26.4 us; the launch traced here: 26.2 us
  starting transfers between devices  12.9 us (49%)
  Pallas kernels  8.58 us (32%)
  waiting for transfers between devices  3.25 us (12%)
  between operations  1.43 us (5%)
    ppermute x3, starting transfers between devices, swap(): lax.ppermute(x, axis, [(i, i ^ bit) for i in range(lax.axis_size(axis))])  6.01 us
    all_to_all x1, starting transfers between devices, exchange_all(): lax.all_to_all(send, ('samples', 'chip', 'core'), 0, 0, axis_index_groups...  3.62 us
    ppermute x3, starting transfers between devices, shift(): return lax.ppermute(x, axis, [(i, (i + step) % size) for i in range(size)])  3.29 us
    pallas_call x1, Pallas kernels, body(): call(functools.partial(slot_hidden_kernel, spread), 8, (jax.ShapeDtypeStr...  2.27 us
    pallas_call x1, Pallas kernels, body(): call(solve_kernel, 9, (jax.ShapeDtypeStruct((2, here), F32),) * 2, name='...  2.16 us
    ppermute x3, waiting for transfers between devices, swap(): lax.ppermute(x, axis, [(i, i ^ bit) for i in range(lax.axis_size(axis))])  2.12 us
    pallas_call x1, Pallas kernels, body(): call(functools.partial(slot_energy_kernel, tuple(shifts)), 5 + len(shifts...  1.93 us
    pallas_call x1, Pallas kernels, body(): call(far_half_kernel, 6, (block,) * 3 + slopes, name='far_half', flops=2...  1.15 us
  transfers between devices with their start and end apart: 7, of which 2 were waited for; matrix products, arithmetic and copies ran while one was open for 0% of the time, Pallas kernels for 24%

profile of v3, /device:TPU:0, one launch (start us, length us, event | category | flops | bytes accessed | tf_op | source)
XLA Modules:
  0.0 26.2 jit_solution(13053641834460213435)
XLA Ops:
  0.6 3.0 %collective-permute-start = (bf16[256,256]{1,0:T(8,128)(2,1)}, bf16[256,256]{1,0:T(8,128)(2,1)S(1)}, u32[]{:S(2)}, u32[]{:S(2)}) collective-permute-start(bf16[256,256]{1,0:T(8,128)(2,1)} %own_hbm.1), channel_id=1, source_target_pairs={{0,2},{2,0},{1,3},{3,1},{4,6},{6,4},{5,7},{7,5},{8,10},{10,8},{9,1... | collective-permute-start | bytes 393224 | tf_op jit(solution)/shard_map/ppermute | solution.py:384
  3.6 0.0 collective-permute-start.1
  3.6 1.5 %collective-permute-start.3 = (s32[1,64,152]{2,1,0:T(8,128)}, s32[1,64,152]{2,1,0:T(8,128)S(1)}, u32[]{:S(2)}, u32[]{:S(2)}) collective-permute-start(s32[1,64,152]{2,1,0:T(8,128)} %bitcast.6), channel_id=1, source_target_pairs={{0,4},{4,0},{8,12},{12,8},{16,20},{20,16},{24,28},{28,24},{1,5},{5... | collective-permute-start | bytes 116744 | tf_op jit(solution)/shard_map/ppermute | solution.py:379
  5.9 2.3 %slot_hidden.1 = (bf16[832,1024]{1,0:T(8,128)(2,1)S(1)}, bf16[64,768]{1,0:T(8,128)(2,1)S(1)}, f32[2,768]{1,0:T(2,128)S(1)}, bf16[152,1024]{1,0:T(8,128)(2,1)S(1)...) custom-call(s32[1,64]{1,0:T(1,128)} %bitcast.8, ...), custom_call_target="tpu_custom_call" | custom-call | flops 258998272 | bytes 2276352 | tf_op jit(solution)/shard_map/slot_hidden/pallas_call | solution.py:438
  8.2 0.0 collective-permute-done.refs_0_
  8.2 0.3 %collective-permute-start.2 = (bf16[256,256]{1,0:T(8,128)(2,1)S(1)}, bf16[256,256]{1,0:T(8,128)(2,1)S(1)}, u32[]{:S(2)}, u32[]{:S(2)}) collective-permute-start(bf16[256,256]{1,0:T(8,128)(2,1)S(1)} %collective-permute-done.refs_0_), channel_id=1, source_target_pairs={{0,1},{1,0},{2,3},{3,2},{4,5},{5,4},{6,7},{7,6},{8,9},{9,8},{10,11... | collective-permute-start | bytes 393224 | tf_op jit(solution)/shard_map/ppermute | solution.py:384
  8.5 0.0 collective-permute-done.3
  8.5 2.7 %collective-permute-start.4 = (bf16[2,64,152]{2,1,0:T(8,128)(2,1)S(1)}, bf16[2,64,152]{2,1,0:T(8,128)(2,1)S(1)}, u32[]{:S(2)}, u32[]{:S(2)}) collective-permute-start(bf16[2,64,152]{2,1,0:T(8,128)(2,1)S(1)} %pad_maximum_fusion.mine_ref), channel_id=1, source_target_pairs={{0,16},{4,20},{8,24},{12,28},{16,0},{20,4},{24,8},{28,12},{1,17},{... | collective-permute-start | bytes 116744 | tf_op jit(solution)/shard_map/ppermute | solution.py:379
  11.2 0.0 collective-permute-done.1.refs_1_
  11.2 0.0 collective-permute-done.2.refs_2_
  11.2 1.9 %slot_energy.1 = (f32[32,1,128]{2,1,0:T(1,128)}, bf16[1024,256]{1,0:T(8,128)(2,1)S(1)}) custom-call(f32[1,1]{1,0:T(1,128)} %bitcast.2.field_ref, bf16[832,1024]{1,0:T(8,128)(2,1)S(1)} %get-tuple-element.27.hidden_ref, bf16[64,768]{1,0:T(8,128)(2,1)S(1)} %get-tuple-element.28.owner_ref, f32[2,768]{1,0:T(2,128)S(1)} %get-tuple-element.29.elements_ref, ...), custom_call_target="tpu_custom_call" | custom-call | flops 436207616 | bytes 540672 | tf_op jit(solution)/shard_map/slot_energy/pallas_call | solution.py:484
  13.1 3.6 %all-to-all-start = ((f32[32,1,128]{2,1,0:T(1,128)}), f32[32,1,128]{2,1,0:T(1,128)S(1)}, u32[]{:S(2)}, u32[]{:S(2)}) async-start(f32[32,1,128]{2,1,0:T(1,128)} %get-tuple-element.33), calls=%async_computation | async-start | bytes 32768 | tf_op jit(solution)/shard_map/all_to_all | solution.py:389
  16.7 0.0 collective-permute-done.4.moved_ref
  16.7 0.1 pack.1.packed_ref
  16.8 1.8 %collective-permute-start.5 = (bf16[320,128]{1,0:T(8,128)(2,1)S(1)}, bf16[320,128]{1,0:T(8,128)(2,1)S(1)}, u32[]{:S(2)}, u32[]{:S(2)}) collective-permute-start(bf16[320,128]{1,0:T(8,128)(2,1)S(1)} %pack.1.packed_ref), channel_id=1, source_target_pairs={{0,8},{4,12},{8,0},{12,4},{16,24},{20,28},{24,16},{28,20},{1,9},{5... | collective-permute-start | bytes 245768 | tf_op jit(solution)/shard_map/ppermute | solution.py:379
  18.7 0.9 %near_half.1 = (bf16[152,1024]{1,0:T(8,128)(2,1)S(1)}, bf16[256,1024]{1,0:T(8,128)(2,1)S(1)}, bf16[768,256]{1,0:T(8,128)(2,1)S(1)}, f32[256,256]{1,0:T(8,128)S(1)}, f32[256,256]{1,0:T(8,128)S(1)}) custom-call(bf16[320,128]{1,0:T(8,128)(2,1)S(1)} %pack.1.packed_ref, bf16[152,1024]{1,0:T(8,128)(2,1)S(1)} %get-tuple-element.36.w1_ref, ...), custom_call_target="tpu_custom_call" | custom-call | flops 10000000000 | bytes 1753088 | tf_op jit(solution)/shard_map/near_half/pallas_call | solution.py:526
  19.6 2.1 %collective-permute-done.5.packed_ref = bf16[320,128]{1,0:T(8,128)(2,1)S(1)} collective-permute-done((bf16[320,128]{1,0:T(8,128)(2,1)S(1)}, bf16[320,128]{1,0:T(8,128)(2,1)S(1)}, u32[]{:S(2)}, u32[]{:S(2)}) %collective-permute-start.5) | collective-permute-done | bytes 81952 | tf_op jit(solution)/shard_map/ppermute | solution.py:379
  21.7 1.2 %far_half.1 = (bf16[768,256]{1,0:T(8,128)(2,1)S(1)}, bf16[768,256]{1,0:T(8,128)(2,1)S(1)}, bf16[768,256]{1,0:T(8,128)(2,1)S(1)}, f32[256,256]{1,0:T(8,128)S(1)}, f32[256,256]{1,0:T(8,128)S(1)}) custom-call(bf16[320,128]{1,0:T(8,128)(2,1)S(1)} %collective-permute-done.5.packed_ref, bf16[152,1024]{1,0:T(8,128)(2,1)S(1)} %get-tuple-element.38.w1_ref, ...), custom_call_target="tpu_custom_call" | custom-call | flops 616562688 | bytes 1703936 | tf_op jit(solution)/shard_map/far_half/pallas_call | solution.py:534
  22.8 1.1 %all-to-all-done.received_ref = f32[32,1,128]{2,1,0:T(1,128)S(1)} async-done(((f32[32,1,128]{2,1,0:T(1,128)}), f32[32,1,128]{2,1,0:T(1,128)S(1)}, u32[]{:S(2)}, u32[]{:S(2)}) %all-to-all-start) | async-done | bytes 16416 | tf_op jit(solution)/shard_map/all_to_all | solution.py:389
  23.9 0.1 collect.1.energy_ref
  24.0 2.2 %solve.1 = (f32[2,64]{1,0:T(2,128)}, f32[2,64]{1,0:T(2,128)}) custom-call(f32[2,512]{1,0:T(2,128)S(1)} %collect.1.energy_ref, bf16[768,256]{1,0:T(8,128)(2,1)S(1)} %get-tuple-element.41.near_ref, f32[256,256]{1,0:T(8,128)S(1)} %get-tuple-element.42.near_re_ref, f32[256,256]{1,0:T(8,128)S(1)} %get-tuple-element.43.near_im_ref, ...), custom_call_target="tpu_custom_call" | custom-call | flops 805306368 | bytes 1024 | tf_op jit(solution)/shard_map/solve/pallas_call | solution.py:542
  (2 shorter events, 0.0 us)
Async XLA Ops:
  0.6 7.5 %collective-permute-start = (bf16[256,256]{1,0:T(8,128)(2,1)}, bf16[256,256]{1,0:T(8,128)(2,1)S(1)}, u32[]{:S(2)}, u32[]{:S(2)}) collective-permute-start(bf16[256,256]{1,0:T(8,128)(2,1)} %own_hbm.1), channel_id=1, source_target_pairs={{0,2},{2,0},{1,3},{3,1},{4,6},{6,4},{5,7},{7,5},{8,10},{10,8},{9,1... | collective-permute-start | bytes 393224 | tf_op jit(solution)/shard_map/ppermute | solution.py:384
  3.6 7.5 %collective-permute-start.1 = (bf16[256,256]{1,0:T(8,128)(2,1)}, bf16[256,256]{1,0:T(8,128)(2,1)S(1)}, u32[]{:S(2)}, u32[]{:S(2)}) collective-permute-start(bf16[256,256]{1,0:T(8,128)(2,1)} %own_hbm.1), channel_id=1, source_target_pairs={{0,1},{1,0},{2,3},{3,2},{4,5},{5,4},{6,7},{7,6},{8,9},{9,8},{10,11... | collective-permute-start | bytes 393224 | tf_op jit(solution)/shard_map/ppermute | solution.py:384
  3.6 4.8 %collective-permute-start.3 = (s32[1,64,152]{2,1,0:T(8,128)}, s32[1,64,152]{2,1,0:T(8,128)S(1)}, u32[]{:S(2)}, u32[]{:S(2)}) collective-permute-start(s32[1,64,152]{2,1,0:T(8,128)} %bitcast.6), channel_id=1, source_target_pairs={{0,4},{4,0},{8,12},{12,8},{16,20},{20,16},{24,28},{28,24},{1,5},{5... | collective-permute-start | bytes 116744 | tf_op jit(solution)/shard_map/ppermute | solution.py:379
  8.2 3.0 %collective-permute-start.2 = (bf16[256,256]{1,0:T(8,128)(2,1)S(1)}, bf16[256,256]{1,0:T(8,128)(2,1)S(1)}, u32[]{:S(2)}, u32[]{:S(2)}) collective-permute-start(bf16[256,256]{1,0:T(8,128)(2,1)S(1)} %collective-permute-done.refs_0_), channel_id=1, source_target_pairs={{0,1},{1,0},{2,3},{3,2},{4,5},{5,4},{6,7},{7,6},{8,9},{9,8},{10,11... | collective-permute-start | bytes 393224 | tf_op jit(solution)/shard_map/ppermute | solution.py:384
  8.5 8.2 %collective-permute-start.4 = (bf16[2,64,152]{2,1,0:T(8,128)(2,1)S(1)}, bf16[2,64,152]{2,1,0:T(8,128)(2,1)S(1)}, u32[]{:S(2)}, u32[]{:S(2)}) collective-permute-start(bf16[2,64,152]{2,1,0:T(8,128)(2,1)S(1)} %pad_maximum_fusion.mine_ref), channel_id=1, source_target_pairs={{0,16},{4,20},{8,24},{12,28},{16,0},{20,4},{24,8},{28,12},{1,17},{... | collective-permute-start | bytes 116744 | tf_op jit(solution)/shard_map/ppermute | solution.py:379
  13.1 10.9 %all-to-all-start = ((f32[32,1,128]{2,1,0:T(1,128)}), f32[32,1,128]{2,1,0:T(1,128)S(1)}, u32[]{:S(2)}, u32[]{:S(2)}) async-start(f32[32,1,128]{2,1,0:T(1,128)} %get-tuple-element.33), calls=%async_computation | async-start | bytes 32768 | tf_op jit(solution)/shard_map/all_to_all | solution.py:389
  16.8 4.8 %collective-permute-start.5 = (bf16[320,128]{1,0:T(8,128)(2,1)S(1)}, bf16[320,128]{1,0:T(8,128)(2,1)S(1)}, u32[]{:S(2)}, u32[]{:S(2)}) collective-permute-start(bf16[320,128]{1,0:T(8,128)(2,1)S(1)} %pack.1.packed_ref), channel_id=1, source_target_pairs={{0,8},{4,12},{8,0},{12,4},{16,24},{20,28},{24,16},{28,20},{1,9},{5... | collective-permute-start | bytes 245768 | tf_op jit(solution)/shard_map/ppermute | solution.py:379

commit v4 on v3

--- a/solution.py
+++ b/solution.py
@@ -161,7 +161,7 @@
         rows = shard.shape[0]
         source = lax.rem(chip + chips - step, chips) * 2 + (core ^ other)
         second_ref[pl.ds(pl.multiple_of(source * rows, rows), rows), :] = shard[...]
-    mid = jnp.tanh(dot(second_ref[...], hidden_ref[...], ((0,), (1,))))
+    mid = jnp.tanh(dot(hidden_ref[...], second_ref[...], ((1,), (0,)))).T
     readout = readout_ref[...].T
     logs_re = jnp.sum(mid * readout[:, 0:1], axis=0, keepdims=True)
     logs_im = jnp.sum(mid * readout[:, 1:2], axis=0, keepdims=True)

time: 26.4 us -> 26.4 us (level)
  no operation moved by 1% of the time
where the time goes in v4:
time: 26.4 us; the launch traced here: 26.1 us
  starting transfers between devices  12.9 us (49%)
  Pallas kernels  8.53 us (32%)
  waiting for transfers between devices  3.23 us (12%)
  between operations  1.43 us (5%)
    ppermute x3, starting transfers between devices, swap(): lax.ppermute(x, axis, [(i, i ^ bit) for i in range(lax.axis_size(axis))])  6.01 us
    all_to_all x1, starting transfers between devices, exchange_all(): lax.all_to_all(send, ('samples', 'chip', 'core'), 0, 0, axis_index_groups...  3.62 us
    ppermute x3, starting transfers between devices, shift(): return lax.ppermute(x, axis, [(i, (i + step) % size) for i in range(size)])  3.29 us
    pallas_call x1, Pallas kernels, body(): call(functools.partial(slot_hidden_kernel, spread), 8, (jax.ShapeDtypeStr...  2.27 us
    pallas_call x1, Pallas kernels, body(): call(solve_kernel, 9, (jax.ShapeDtypeStruct((2, here), F32),) * 2, name='...  2.17 us
    ppermute x3, waiting for transfers between devices, swap(): lax.ppermute(x, axis, [(i, i ^ bit) for i in range(lax.axis_size(axis))])  2.12 us
    pallas_call x1, Pallas kernels, body(): call(functools.partial(slot_energy_kernel, tuple(shifts)), 5 + len(shifts...  1.85 us
    pallas_call x1, Pallas kernels, body(): call(far_half_kernel, 6, (block,) * 3 + slopes, name='far_half', flops=2...  1.17 us
  transfers between devices with their start and end apart: 7, of which 2 were waited for; matrix products, arithmetic and copies ran while one was open for 0% of the time, Pallas kernels for 24%

profile of v4, /device:TPU:0, one launch (start us, length us, event | category | flops | bytes accessed | tf_op | source)
XLA Modules:
  0.0 26.1 jit_solution(11262870626313794438)
XLA Ops:
  0.6 3.0 %collective-permute-start = (bf16[256,256]{1,0:T(8,128)(2,1)}, bf16[256,256]{1,0:T(8,128)(2,1)S(1)}, u32[]{:S(2)}, u32[]{:S(2)}) collective-permute-start(bf16[256,256]{1,0:T(8,128)(2,1)} %own_hbm.1), channel_id=1, source_target_pairs={{0,2},{2,0},{1,3},{3,1},{4,6},{6,4},{5,7},{7,5},{8,10},{10,8},{9,1... | collective-permute-start | bytes 393224 | tf_op jit(solution)/shard_map/ppermute | solution.py:384
  3.6 0.0 collective-permute-start.1
  3.6 1.5 %collective-permute-start.3 = (s32[1,64,152]{2,1,0:T(8,128)}, s32[1,64,152]{2,1,0:T(8,128)S(1)}, u32[]{:S(2)}, u32[]{:S(2)}) collective-permute-start(s32[1,64,152]{2,1,0:T(8,128)} %bitcast.6), channel_id=1, source_target_pairs={{0,4},{4,0},{8,12},{12,8},{16,20},{20,16},{24,28},{28,24},{1,5},{5... | collective-permute-start | bytes 116744 | tf_op jit(solution)/shard_map/ppermute | solution.py:379
  5.9 2.3 %slot_hidden.1 = (bf16[832,1024]{1,0:T(8,128)(2,1)S(1)}, bf16[64,768]{1,0:T(8,128)(2,1)S(1)}, f32[2,768]{1,0:T(2,128)S(1)}, bf16[152,1024]{1,0:T(8,128)(2,1)S(1)...) custom-call(s32[1,64]{1,0:T(1,128)} %bitcast.8, ...), custom_call_target="tpu_custom_call" | custom-call | flops 258998272 | bytes 2276352 | tf_op jit(solution)/shard_map/slot_hidden/pallas_call | solution.py:438
  8.2 0.0 collective-permute-done.refs_0_
  8.2 0.3 %collective-permute-start.2 = (bf16[256,256]{1,0:T(8,128)(2,1)S(1)}, bf16[256,256]{1,0:T(8,128)(2,1)S(1)}, u32[]{:S(2)}, u32[]{:S(2)}) collective-permute-start(bf16[256,256]{1,0:T(8,128)(2,1)S(1)} %collective-permute-done.refs_0_), channel_id=1, source_target_pairs={{0,1},{1,0},{2,3},{3,2},{4,5},{5,4},{6,7},{7,6},{8,9},{9,8},{10,11... | collective-permute-start | bytes 393224 | tf_op jit(solution)/shard_map/ppermute | solution.py:384
  8.5 0.0 collective-permute-done.3
  8.5 2.7 %collective-permute-start.4 = (bf16[2,64,152]{2,1,0:T(8,128)(2,1)S(1)}, bf16[2,64,152]{2,1,0:T(8,128)(2,1)S(1)}, u32[]{:S(2)}, u32[]{:S(2)}) collective-permute-start(bf16[2,64,152]{2,1,0:T(8,128)(2,1)S(1)} %pad_maximum_fusion.mine_ref), channel_id=1, source_target_pairs={{0,16},{4,20},{8,24},{12,28},{16,0},{20,4},{24,8},{28,12},{1,17},{... | collective-permute-start | bytes 116744 | tf_op jit(solution)/shard_map/ppermute | solution.py:379
  11.2 0.0 collective-permute-done.1.refs_1_
  11.2 0.0 collective-permute-done.2.refs_2_
  11.2 1.9 %slot_energy.1 = (f32[32,1,128]{2,1,0:T(1,128)}, bf16[1024,256]{1,0:T(8,128)(2,1)S(1)}) custom-call(f32[1,1]{1,0:T(1,128)} %bitcast.2.field_ref, bf16[832,1024]{1,0:T(8,128)(2,1)S(1)} %get-tuple-element.27.hidden_ref, bf16[64,768]{1,0:T(8,128)(2,1)S(1)} %get-tuple-element.28.owner_ref, f32[2,768]{1,0:T(2,128)S(1)} %get-tuple-element.29.elements_ref, ...), custom_call_target="tpu_custom_call" | custom-call | flops 436207616 | bytes 540672 | tf_op jit(solution)/shard_map/slot_energy/pallas_call | solution.py:484
  13.0 3.6 %all-to-all-start = ((f32[32,1,128]{2,1,0:T(1,128)}), f32[32,1,128]{2,1,0:T(1,128)S(1)}, u32[]{:S(2)}, u32[]{:S(2)}) async-start(f32[32,1,128]{2,1,0:T(1,128)} %get-tuple-element.33), calls=%async_computation | async-start | bytes 32768 | tf_op jit(solution)/shard_map/all_to_all | solution.py:389
  16.6 0.0 collective-permute-done.4.moved_ref
  16.7 0.1 pack.1.packed_ref
  16.8 1.8 %collective-permute-start.5 = (bf16[320,128]{1,0:T(8,128)(2,1)S(1)}, bf16[320,128]{1,0:T(8,128)(2,1)S(1)}, u32[]{:S(2)}, u32[]{:S(2)}) collective-permute-start(bf16[320,128]{1,0:T(8,128)(2,1)S(1)} %pack.1.packed_ref), channel_id=1, source_target_pairs={{0,8},{4,12},{8,0},{12,4},{16,24},{20,28},{24,16},{28,20},{1,9},{5... | collective-permute-start | bytes 245768 | tf_op jit(solution)/shard_map/ppermute | solution.py:379
  18.6 0.9 %near_half.1 = (bf16[152,1024]{1,0:T(8,128)(2,1)S(1)}, bf16[256,1024]{1,0:T(8,128)(2,1)S(1)}, bf16[768,256]{1,0:T(8,128)(2,1)S(1)}, f32[256,256]{1,0:T(8,128)S(1)}, f32[256,256]{1,0:T(8,128)S(1)}) custom-call(bf16[320,128]{1,0:T(8,128)(2,1)S(1)} %pack.1.packed_ref, bf16[152,1024]{1,0:T(8,128)(2,1)S(1)} %get-tuple-element.36.w1_ref, ...), custom_call_target="tpu_custom_call" | custom-call | flops 10000000000 | bytes 1753088 | tf_op jit(solution)/shard_map/near_half/pallas_call | solution.py:526
  19.5 2.1 %collective-permute-done.5.packed_ref = bf16[320,128]{1,0:T(8,128)(2,1)S(1)} collective-permute-done((bf16[320,128]{1,0:T(8,128)(2,1)S(1)}, bf16[320,128]{1,0:T(8,128)(2,1)S(1)}, u32[]{:S(2)}, u32[]{:S(2)}) %collective-permute-start.5) | collective-permute-done | bytes 81952 | tf_op jit(solution)/shard_map/ppermute | solution.py:379
  21.6 1.2 %far_half.1 = (bf16[768,256]{1,0:T(8,128)(2,1)S(1)}, bf16[768,256]{1,0:T(8,128)(2,1)S(1)}, bf16[768,256]{1,0:T(8,128)(2,1)S(1)}, f32[256,256]{1,0:T(8,128)S(1)}, f32[256,256]{1,0:T(8,128)S(1)}) custom-call(bf16[320,128]{1,0:T(8,128)(2,1)S(1)} %collective-permute-done.5.packed_ref, bf16[152,1024]{1,0:T(8,128)(2,1)S(1)} %get-tuple-element.38.w1_ref, ...), custom_call_target="tpu_custom_call" | custom-call | flops 616562688 | bytes 1703936 | tf_op jit(solution)/shard_map/far_half/pallas_call | solution.py:534
  22.8 1.1 %all-to-all-done.received_ref = f32[32,1,128]{2,1,0:T(1,128)S(1)} async-done(((f32[32,1,128]{2,1,0:T(1,128)}), f32[32,1,128]{2,1,0:T(1,128)S(1)}, u32[]{:S(2)}, u32[]{:S(2)}) %all-to-all-start) | async-done | bytes 16416 | tf_op jit(solution)/shard_map/all_to_all | solution.py:389
  23.9 0.1 collect.1.energy_ref
  24.0 2.2 %solve.1 = (f32[2,64]{1,0:T(2,128)}, f32[2,64]{1,0:T(2,128)}) custom-call(f32[2,512]{1,0:T(2,128)S(1)} %collect.1.energy_ref, bf16[768,256]{1,0:T(8,128)(2,1)S(1)} %get-tuple-element.41.near_ref, f32[256,256]{1,0:T(8,128)S(1)} %get-tuple-element.42.near_re_ref, f32[256,256]{1,0:T(8,128)S(1)} %get-tuple-element.43.near_im_ref, ...), custom_call_target="tpu_custom_call" | custom-call | flops 805306368 | bytes 1024 | tf_op jit(solution)/shard_map/solve/pallas_call | solution.py:542
  (2 shorter events, 0.0 us)
Async XLA Ops:
  0.6 7.5 %collective-permute-start = (bf16[256,256]{1,0:T(8,128)(2,1)}, bf16[256,256]{1,0:T(8,128)(2,1)S(1)}, u32[]{:S(2)}, u32[]{:S(2)}) collective-permute-start(bf16[256,256]{1,0:T(8,128)(2,1)} %own_hbm.1), channel_id=1, source_target_pairs={{0,2},{2,0},{1,3},{3,1},{4,6},{6,4},{5,7},{7,5},{8,10},{10,8},{9,1... | collective-permute-start | bytes 393224 | tf_op jit(solution)/shard_map/ppermute | solution.py:384
  3.6 7.5 %collective-permute-start.1 = (bf16[256,256]{1,0:T(8,128)(2,1)}, bf16[256,256]{1,0:T(8,128)(2,1)S(1)}, u32[]{:S(2)}, u32[]{:S(2)}) collective-permute-start(bf16[256,256]{1,0:T(8,128)(2,1)} %own_hbm.1), channel_id=1, source_target_pairs={{0,1},{1,0},{2,3},{3,2},{4,5},{5,4},{6,7},{7,6},{8,9},{9,8},{10,11... | collective-permute-start | bytes 393224 | tf_op jit(solution)/shard_map/ppermute | solution.py:384
  3.6 4.8 %collective-permute-start.3 = (s32[1,64,152]{2,1,0:T(8,128)}, s32[1,64,152]{2,1,0:T(8,128)S(1)}, u32[]{:S(2)}, u32[]{:S(2)}) collective-permute-start(s32[1,64,152]{2,1,0:T(8,128)} %bitcast.6), channel_id=1, source_target_pairs={{0,4},{4,0},{8,12},{12,8},{16,20},{20,16},{24,28},{28,24},{1,5},{5... | collective-permute-start | bytes 116744 | tf_op jit(solution)/shard_map/ppermute | solution.py:379
  8.2 3.0 %collective-permute-start.2 = (bf16[256,256]{1,0:T(8,128)(2,1)S(1)}, bf16[256,256]{1,0:T(8,128)(2,1)S(1)}, u32[]{:S(2)}, u32[]{:S(2)}) collective-permute-start(bf16[256,256]{1,0:T(8,128)(2,1)S(1)} %collective-permute-done.refs_0_), channel_id=1, source_target_pairs={{0,1},{1,0},{2,3},{3,2},{4,5},{5,4},{6,7},{7,6},{8,9},{9,8},{10,11... | collective-permute-start | bytes 393224 | tf_op jit(solution)/shard_map/ppermute | solution.py:384
  8.5 8.2 %collective-permute-start.4 = (bf16[2,64,152]{2,1,0:T(8,128)(2,1)S(1)}, bf16[2,64,152]{2,1,0:T(8,128)(2,1)S(1)}, u32[]{:S(2)}, u32[]{:S(2)}) collective-permute-start(bf16[2,64,152]{2,1,0:T(8,128)(2,1)S(1)} %pad_maximum_fusion.mine_ref), channel_id=1, source_target_pairs={{0,16},{4,20},{8,24},{12,28},{16,0},{20,4},{24,8},{28,12},{1,17},{... | collective-permute-start | bytes 116744 | tf_op jit(solution)/shard_map/ppermute | solution.py:379
  13.0 10.9 %all-to-all-start = ((f32[32,1,128]{2,1,0:T(1,128)}), f32[32,1,128]{2,1,0:T(1,128)S(1)}, u32[]{:S(2)}, u32[]{:S(2)}) async-start(f32[32,1,128]{2,1,0:T(1,128)} %get-tuple-element.33), calls=%async_computation | async-start | bytes 32768 | tf_op jit(solution)/shard_map/all_to_all | solution.py:389
  16.8 4.8 %collective-permute-start.5 = (bf16[320,128]{1,0:T(8,128)(2,1)S(1)}, bf16[320,128]{1,0:T(8,128)(2,1)S(1)}, u32[]{:S(2)}, u32[]{:S(2)}) collective-permute-start(bf16[320,128]{1,0:T(8,128)(2,1)S(1)} %pack.1.packed_ref), channel_id=1, source_target_pairs={{0,8},{4,12},{8,0},{12,4},{16,24},{20,28},{24,16},{28,20},{1,9},{5... | collective-permute-start | bytes 245768 | tf_op jit(solution)/shard_map/ppermute | solution.py:379

commit v5 on v4

--- a/solution.py
+++ b/solution.py
@@ -116,18 +116,16 @@
     copies[3].wait()
     w1 = w1_ref[...]
     bias = bias_ref[...]
-    hidden_ref[slots:, :] = jnp.tanh(dot(occupied, w1, ((1,), (0,))) + bias).astype(BF16)
+    own = occ_ref[...].astype(F32).T
     copies[4].wait()
-    for start in range(0, slots, ROWS):
-        stop = min(start + ROWS, slots)
-        parent_occ = dot(occupied, owner[:, start:stop], ((0,), (0,)))
-        columns = iota((orbitals, stop - start), 0)
-        flipped = columns == orbitals_ref[0:1, start:stop]
-        for u in range(1, updates):
-            flipped = flipped | (columns == orbitals_ref[u : u + 1, start:stop])
-        slot_occ = jnp.where(flipped, 1.0 - parent_occ, parent_occ).astype(BF16)
-        pre = dot(slot_occ, w1, ((0,), (0,))) + bias
-        hidden_ref[start:stop, :] = jnp.tanh(pre).astype(BF16)
+    parent_occ = dot(occupied, owner, ((0,), (0,)))
+    columns = iota((orbitals, slots), 0)
+    flipped = columns == orbitals_ref[0:1, :]
+    for u in range(1, updates):
+        flipped = flipped | (columns == orbitals_ref[u : u + 1, :])
+    slot_occ = jnp.where(flipped, 1.0 - parent_occ, parent_occ)
+    all_occ = jnp.concatenate([slot_occ, own], axis=1).astype(BF16)
+    hidden_ref[...] = jnp.tanh(dot(all_occ, w1, ((0,), (0,))) + bias).astype(BF16)
     copies[5].wait()
     copies[6].wait()
     copies[7].wait()

time: 26.4 us -> 26.4 us (level)
  no operation moved by 1% of the time
where the time goes in v5:
time: 26.4 us; the launch traced here: 26.1 us
  starting transfers between devices  13 us (49%)
  Pallas kernels  8.46 us (32%)
  waiting for transfers between devices  3.23 us (12%)
  between operations  1.43 us (5%)
    ppermute x3, starting transfers between devices, swap(): lax.ppermute(x, axis, [(i, i ^ bit) for i in range(lax.axis_size(axis))])  6.01 us
    all_to_all x1, starting transfers between devices, exchange_all(): lax.all_to_all(send, ('samples', 'chip', 'core'), 0, 0, axis_index_groups...  3.69 us
    ppermute x3, starting transfers between devices, shift(): return lax.ppermute(x, axis, [(i, (i + step) % size) for i in range(size)])  3.3 us
    pallas_call x1, Pallas kernels, body(): call(functools.partial(slot_hidden_kernel, spread), 8, (jax.ShapeDtypeStr...  2.2 us
    pallas_call x1, Pallas kernels, body(): call(solve_kernel, 9, (jax.ShapeDtypeStruct((2, here), F32),) * 2, name='...  2.17 us
    ppermute x3, waiting for transfers between devices, swap(): lax.ppermute(x, axis, [(i, i ^ bit) for i in range(lax.axis_size(axis))])  2.12 us
    pallas_call x1, Pallas kernels, body(): call(functools.partial(slot_energy_kernel, tuple(shifts)), 5 + len(shifts...  1.85 us
    pallas_call x1, Pallas kernels, body(): call(far_half_kernel, 6, (block,) * 3 + slopes, name='far_half', flops=2...  1.17 us
  transfers between devices with their start and end apart: 7, of which 2 were waited for; matrix products, arithmetic and copies ran while one was open for 0% of the time, Pallas kernels for 24%

profile of v5, /device:TPU:0, one launch (start us, length us, event | category | flops | bytes accessed | tf_op | source)
XLA Modules:
  0.0 26.1 jit_solution(228856560411482984)
XLA Ops:
  0.6 3.0 %collective-permute-start = (bf16[256,256]{1,0:T(8,128)(2,1)}, bf16[256,256]{1,0:T(8,128)(2,1)S(1)}, u32[]{:S(2)}, u32[]{:S(2)}) collective-permute-start(bf16[256,256]{1,0:T(8,128)(2,1)} %own_hbm.1), channel_id=1, source_target_pairs={{0,2},{2,0},{1,3},{3,1},{4,6},{6,4},{5,7},{7,5},{8,10},{10,8},{9,1... | collective-permute-start | bytes 393224 | tf_op jit(solution)/shard_map/ppermute | solution.py:382
  3.6 0.0 collective-permute-start.1
  3.6 1.5 %collective-permute-start.3 = (s32[1,64,152]{2,1,0:T(8,128)}, s32[1,64,152]{2,1,0:T(8,128)S(1)}, u32[]{:S(2)}, u32[]{:S(2)}) collective-permute-start(s32[1,64,152]{2,1,0:T(8,128)} %bitcast.6), channel_id=1, source_target_pairs={{0,4},{4,0},{8,12},{12,8},{16,20},{20,16},{24,28},{28,24},{1,5},{5... | collective-permute-start | bytes 116744 | tf_op jit(solution)/shard_map/ppermute | solution.py:377
  5.9 2.2 %slot_hidden.1 = (bf16[832,1024]{1,0:T(8,128)(2,1)S(1)}, bf16[64,768]{1,0:T(8,128)(2,1)S(1)}, f32[2,768]{1,0:T(2,128)S(1)}, bf16[152,1024]{1,0:T(8,128)(2,1)S(1)...) custom-call(s32[1,64]{1,0:T(1,128)} %bitcast.8, ...), custom_call_target="tpu_custom_call" | custom-call | flops 258998272 | bytes 2276352 | tf_op jit(solution)/shard_map/slot_hidden/pallas_call | solution.py:436
  8.1 0.0 collective-permute-done.refs_0_
  8.1 0.3 %collective-permute-start.2 = (bf16[256,256]{1,0:T(8,128)(2,1)S(1)}, bf16[256,256]{1,0:T(8,128)(2,1)S(1)}, u32[]{:S(2)}, u32[]{:S(2)}) collective-permute-start(bf16[256,256]{1,0:T(8,128)(2,1)S(1)} %collective-permute-done.refs_0_), channel_id=1, source_target_pairs={{0,1},{1,0},{2,3},{3,2},{4,5},{5,4},{6,7},{7,6},{8,9},{9,8},{10,11... | collective-permute-start | bytes 393224 | tf_op jit(solution)/shard_map/ppermute | solution.py:382
  8.4 0.0 collective-permute-done.3
  8.4 2.7 %collective-permute-start.4 = (bf16[2,64,152]{2,1,0:T(8,128)(2,1)S(1)}, bf16[2,64,152]{2,1,0:T(8,128)(2,1)S(1)}, u32[]{:S(2)}, u32[]{:S(2)}) collective-permute-start(bf16[2,64,152]{2,1,0:T(8,128)(2,1)S(1)} %pad_maximum_fusion.mine_ref), channel_id=1, source_target_pairs={{0,16},{4,20},{8,24},{12,28},{16,0},{20,4},{24,8},{28,12},{1,17},{... | collective-permute-start | bytes 116744 | tf_op jit(solution)/shard_map/ppermute | solution.py:377
  11.1 0.0 collective-permute-done.1.refs_1_
  11.1 0.0 collective-permute-done.2.refs_2_
  11.1 1.9 %slot_energy.1 = (f32[32,1,128]{2,1,0:T(1,128)}, bf16[1024,256]{1,0:T(8,128)(2,1)S(1)}) custom-call(f32[1,1]{1,0:T(1,128)} %bitcast.2.field_ref, bf16[832,1024]{1,0:T(8,128)(2,1)S(1)} %get-tuple-element.27.hidden_ref, bf16[64,768]{1,0:T(8,128)(2,1)S(1)} %get-tuple-element.28.owner_ref, f32[2,768]{1,0:T(2,128)S(1)} %get-tuple-element.29.elements_ref, ...), custom_call_target="tpu_custom_call" | custom-call | flops 436207616 | bytes 540672 | tf_op jit(solution)/shard_map/slot_energy/pallas_call | solution.py:482
  13.0 3.7 %all-to-all-start = ((f32[32,1,128]{2,1,0:T(1,128)}), f32[32,1,128]{2,1,0:T(1,128)S(1)}, u32[]{:S(2)}, u32[]{:S(2)}) async-start(f32[32,1,128]{2,1,0:T(1,128)} %get-tuple-element.33), calls=%async_computation | async-start | bytes 32768 | tf_op jit(solution)/shard_map/all_to_all | solution.py:387
  16.6 0.0 collective-permute-done.4.moved_ref
  16.7 0.1 pack.1.packed_ref
  16.8 1.8 %collective-permute-start.5 = (bf16[320,128]{1,0:T(8,128)(2,1)S(1)}, bf16[320,128]{1,0:T(8,128)(2,1)S(1)}, u32[]{:S(2)}, u32[]{:S(2)}) collective-permute-start(bf16[320,128]{1,0:T(8,128)(2,1)S(1)} %pack.1.packed_ref), channel_id=1, source_target_pairs={{0,8},{4,12},{8,0},{12,4},{16,24},{20,28},{24,16},{28,20},{1,9},{5... | collective-permute-start | bytes 245768 | tf_op jit(solution)/shard_map/ppermute | solution.py:377
  18.6 0.9 %near_half.1 = (bf16[152,1024]{1,0:T(8,128)(2,1)S(1)}, bf16[256,1024]{1,0:T(8,128)(2,1)S(1)}, bf16[768,256]{1,0:T(8,128)(2,1)S(1)}, f32[256,256]{1,0:T(8,128)S(1)}, f32[256,256]{1,0:T(8,128)S(1)}) custom-call(bf16[320,128]{1,0:T(8,128)(2,1)S(1)} %pack.1.packed_ref, bf16[152,1024]{1,0:T(8,128)(2,1)S(1)} %get-tuple-element.36.w1_ref, ...), custom_call_target="tpu_custom_call" | custom-call | flops 10000000000 | bytes 1753088 | tf_op jit(solution)/shard_map/near_half/pallas_call | solution.py:524
  19.5 2.1 %collective-permute-done.5.packed_ref = bf16[320,128]{1,0:T(8,128)(2,1)S(1)} collective-permute-done((bf16[320,128]{1,0:T(8,128)(2,1)S(1)}, bf16[320,128]{1,0:T(8,128)(2,1)S(1)}, u32[]{:S(2)}, u32[]{:S(2)}) %collective-permute-start.5) | collective-permute-done | bytes 81952 | tf_op jit(solution)/shard_map/ppermute | solution.py:377
  21.6 1.2 %far_half.1 = (bf16[768,256]{1,0:T(8,128)(2,1)S(1)}, bf16[768,256]{1,0:T(8,128)(2,1)S(1)}, bf16[768,256]{1,0:T(8,128)(2,1)S(1)}, f32[256,256]{1,0:T(8,128)S(1)}, f32[256,256]{1,0:T(8,128)S(1)}) custom-call(bf16[320,128]{1,0:T(8,128)(2,1)S(1)} %collective-permute-done.5.packed_ref, bf16[152,1024]{1,0:T(8,128)(2,1)S(1)} %get-tuple-element.38.w1_ref, ...), custom_call_target="tpu_custom_call" | custom-call | flops 616562688 | bytes 1703936 | tf_op jit(solution)/shard_map/far_half/pallas_call | solution.py:532
  22.8 1.1 %all-to-all-done.received_ref = f32[32,1,128]{2,1,0:T(1,128)S(1)} async-done(((f32[32,1,128]{2,1,0:T(1,128)}), f32[32,1,128]{2,1,0:T(1,128)S(1)}, u32[]{:S(2)}, u32[]{:S(2)}) %all-to-all-start) | async-done | bytes 16416 | tf_op jit(solution)/shard_map/all_to_all | solution.py:387
  23.9 0.1 collect.1.energy_ref
  24.0 2.2 %solve.1 = (f32[2,64]{1,0:T(2,128)}, f32[2,64]{1,0:T(2,128)}) custom-call(f32[2,512]{1,0:T(2,128)S(1)} %collect.1.energy_ref, bf16[768,256]{1,0:T(8,128)(2,1)S(1)} %get-tuple-element.41.near_ref, f32[256,256]{1,0:T(8,128)S(1)} %get-tuple-element.42.near_re_ref, f32[256,256]{1,0:T(8,128)S(1)} %get-tuple-element.43.near_im_ref, ...), custom_call_target="tpu_custom_call" | custom-call | flops 805306368 | bytes 1024 | tf_op jit(solution)/shard_map/solve/pallas_call | solution.py:540
  (2 shorter events, 0.0 us)
Async XLA Ops:
  0.6 7.5 %collective-permute-start = (bf16[256,256]{1,0:T(8,128)(2,1)}, bf16[256,256]{1,0:T(8,128)(2,1)S(1)}, u32[]{:S(2)}, u32[]{:S(2)}) collective-permute-start(bf16[256,256]{1,0:T(8,128)(2,1)} %own_hbm.1), channel_id=1, source_target_pairs={{0,2},{2,0},{1,3},{3,1},{4,6},{6,4},{5,7},{7,5},{8,10},{10,8},{9,1... | collective-permute-start | bytes 393224 | tf_op jit(solution)/shard_map/ppermute | solution.py:382
  3.6 7.5 %collective-permute-start.1 = (bf16[256,256]{1,0:T(8,128)(2,1)}, bf16[256,256]{1,0:T(8,128)(2,1)S(1)}, u32[]{:S(2)}, u32[]{:S(2)}) collective-permute-start(bf16[256,256]{1,0:T(8,128)(2,1)} %own_hbm.1), channel_id=1, source_target_pairs={{0,1},{1,0},{2,3},{3,2},{4,5},{5,4},{6,7},{7,6},{8,9},{9,8},{10,11... | collective-permute-start | bytes 393224 | tf_op jit(solution)/shard_map/ppermute | solution.py:382
  3.6 4.8 %collective-permute-start.3 = (s32[1,64,152]{2,1,0:T(8,128)}, s32[1,64,152]{2,1,0:T(8,128)S(1)}, u32[]{:S(2)}, u32[]{:S(2)}) collective-permute-start(s32[1,64,152]{2,1,0:T(8,128)} %bitcast.6), channel_id=1, source_target_pairs={{0,4},{4,0},{8,12},{12,8},{16,20},{20,16},{24,28},{28,24},{1,5},{5... | collective-permute-start | bytes 116744 | tf_op jit(solution)/shard_map/ppermute | solution.py:377
  8.1 3.0 %collective-permute-start.2 = (bf16[256,256]{1,0:T(8,128)(2,1)S(1)}, bf16[256,256]{1,0:T(8,128)(2,1)S(1)}, u32[]{:S(2)}, u32[]{:S(2)}) collective-permute-start(bf16[256,256]{1,0:T(8,128)(2,1)S(1)} %collective-permute-done.refs_0_), channel_id=1, source_target_pairs={{0,1},{1,0},{2,3},{3,2},{4,5},{5,4},{6,7},{7,6},{8,9},{9,8},{10,11... | collective-permute-start | bytes 393224 | tf_op jit(solution)/shard_map/ppermute | solution.py:382
  8.4 8.2 %collective-permute-start.4 = (bf16[2,64,152]{2,1,0:T(8,128)(2,1)S(1)}, bf16[2,64,152]{2,1,0:T(8,128)(2,1)S(1)}, u32[]{:S(2)}, u32[]{:S(2)}) collective-permute-start(bf16[2,64,152]{2,1,0:T(8,128)(2,1)S(1)} %pad_maximum_fusion.mine_ref), channel_id=1, source_target_pairs={{0,16},{4,20},{8,24},{12,28},{16,0},{20,4},{24,8},{28,12},{1,17},{... | collective-permute-start | bytes 116744 | tf_op jit(solution)/shard_map/ppermute | solution.py:377
  13.0 10.9 %all-to-all-start = ((f32[32,1,128]{2,1,0:T(1,128)}), f32[32,1,128]{2,1,0:T(1,128)S(1)}, u32[]{:S(2)}, u32[]{:S(2)}) async-start(f32[32,1,128]{2,1,0:T(1,128)} %get-tuple-element.33), calls=%async_computation | async-start | bytes 32768 | tf_op jit(solution)/shard_map/all_to_all | solution.py:387
  16.8 4.8 %collective-permute-start.5 = (bf16[320,128]{1,0:T(8,128)(2,1)S(1)}, bf16[320,128]{1,0:T(8,128)(2,1)S(1)}, u32[]{:S(2)}, u32[]{:S(2)}) collective-permute-start(bf16[320,128]{1,0:T(8,128)(2,1)S(1)} %pack.1.packed_ref), channel_id=1, source_target_pairs={{0,8},{4,12},{8,0},{12,4},{16,24},{20,28},{24,16},{28,20},{1,9},{5... | collective-permute-start | bytes 245768 | tf_op jit(solution)/shard_map/ppermute | solution.py:377
